TPU v7x, 32 devices: a whole 2x2x4 slice. The times are simulated.
32 devices in a mesh: tm: 8 (over z, x), lat: 4 (over y, core).
Axes of the slice: x: 2, y: 2, z: 4, core: 2. Of those that a mesh axis runs over, the one named last changes fastest.
Arguments:
- wind_east: bfloat16 [960, 32, 1440], P('tm', 'lat'), may hold values from -40 to 40
- wind_north: bfloat16 [960, 32, 1440], P('tm', 'lat'), may hold values from -40 to 40
- snap_counts: int32 [8], P('tm'), may hold values from 1 to 120, 320 in all
- snap_ids: int32 [960], P('tm'), may hold values from 0 to 8759
Outputs:
- basis: bfloat16 [32, 32, 1440], P(None, 'lat')
- coeffs: float32 [32, 960], P(None, 'tm')
Inputs may be any that keep to these rules, and one draw needn't show every extreme that they name: `snap_counts`: entry b counts the used slots of the b-th block of 120 slots, which are that block's first ones; the entries sum to 320 and one of them equals 120.
All inputs are finite; a program needn't handle non-finite values.
Results may differ from a plain program's by a relative error of at most 0.0072.
Values may be sent and summed in bfloat16 or wider, within the bound.
No kernel may reach another device: no remote copies, remote signals or barrier semaphores. Data moves between devices by JAX's collectives and lax.ppermute only.
A program may use at most 64 MiB of HBM per device.

v0:
```python
import jax
import jax.numpy as jnp
from jax import lax
from jax.sharding import PartitionSpec as P

RANK = 32


def with_halo(cells, sides, width):
    for axis, dim in sides:
        count = lax.axis_size(axis)
        ends = count - 1
        head = lax.slice_in_dim(cells, 0, width, axis=dim)
        tail = lax.slice_in_dim(cells, cells.shape[dim] - width, cells.shape[dim], axis=dim)
        cells = jnp.concatenate(
            [
                lax.ppermute(tail, axis, [(i, (i + 1) % count) for i in range(ends)]),
                cells,
                lax.ppermute(head, axis, [((i + 1) % count, i) for i in range(ends)]),
            ],
            axis=dim,
        )
    return cells


def latitude_cosine(first_row, row_count, total_rows):
    row_index = first_row + jnp.arange(row_count, dtype=jnp.int32)
    return jnp.cos((total_rows // 2 - row_index).astype(jnp.float32) * (jnp.pi / 720.0))


def sign_table(snap_ids, rank_count):
    column = jnp.arange(rank_count, dtype=jnp.int32)
    mixed = snap_ids[:, None] * 1103515245 + column[None, :] * 40503 + 12345
    mixed = jnp.bitwise_xor(mixed, jnp.right_shift(mixed, 13))
    mixed = mixed * 1664525 + 1013904223
    mixed = jnp.bitwise_xor(mixed, jnp.right_shift(mixed, 16))
    flipped = jnp.bitwise_and(jnp.right_shift(mixed, 7), 1)
    return (1 - 2 * flipped).astype(jnp.bfloat16)


def metric_vorticity(padded_east, wind_north, padded_cosine, valid):
    scaled = padded_east.astype(jnp.float32) * padded_cosine[None, :, None]
    north_side = scaled[:, :-2]
    south_side = scaled[:, 2:]
    meridional = wind_north.astype(jnp.float32)
    zonal_diff = jnp.roll(meridional, -1, axis=2) - jnp.roll(meridional, 1, axis=2)
    weight = 0.5 / jnp.sqrt(padded_cosine[1:-1])
    field = (zonal_diff - north_side + south_side) * weight[None, :, None] * valid[:, None, None]
    return field.astype(jnp.bfloat16)


def local_gram(sketch, cell_total):
    return (
        lax.dot_general(
            sketch,
            sketch,
            (((1,), (1,)), ((), ())),
            precision=lax.Precision.HIGHEST,
            preferred_element_type=jnp.float32,
        )
        / cell_total
    )


def orthonormal(gram_sum, sketch):
    factor = jnp.linalg.cholesky(gram_sum)
    inverse = lax.linalg.triangular_solve(
        factor, jnp.eye(gram_sum.shape[0], dtype=jnp.float32), left_side=True, lower=True
    )
    return jnp.dot(
        inverse, sketch, precision=lax.Precision.HIGHEST, preferred_element_type=jnp.float32
    ).astype(jnp.bfloat16)


def local(wind_east, wind_north, snap_counts, snap_ids):
    snap_slots, band_rows, lon_count = wind_east.shape
    band_count = lax.axis_size("lat")
    first_row = lax.axis_index("lat") * band_rows - 1
    padded_cosine = latitude_cosine(first_row, band_rows + 2, band_rows * band_count)
    valid = (jnp.arange(snap_slots, dtype=jnp.int32) < snap_counts[0]).astype(jnp.float32)
    padded_east = with_halo(wind_east, (("lat", 1),), 1)
    field = metric_vorticity(padded_east, wind_north, padded_cosine, valid).reshape(
        snap_slots, band_rows * lon_count
    )
    signs_matrix = sign_table(snap_ids, RANK)
    sketch = jnp.dot(signs_matrix.T, field, preferred_element_type=jnp.float32)
    cell_total = band_rows * band_count * lon_count
    sketch = lax.psum(sketch, "tm")
    gram_sum = lax.psum(local_gram(sketch, cell_total), "lat")
    basis_flat = orthonormal(gram_sum, sketch)
    projected = (
        lax.dot_general(
            basis_flat, field, (((1,), (1,)), ((), ())), preferred_element_type=jnp.float32
        )
        / cell_total
    )
    coeffs = lax.psum(projected, "lat")
    return (basis_flat.reshape(basis_flat.shape[0], band_rows, lon_count), coeffs)


def solution(mesh):
    in_specs = (P("tm", "lat", None), P("tm", "lat", None), P("tm"), P("tm"))
    out_specs = (P(None, "lat", None), P(None, "tm"))
    return jax.shard_map(local, mesh=mesh, in_specs=in_specs, out_specs=out_specs, check_vma=False)
```

profile of v0, /device:TPU:0, one launch (start us, length us, event | category | flops | bytes accessed | tf_op | source)
XLA Modules:
  0.0 181.5 jit_solution(10604484795392648130)
XLA Ops:
  7.2 0.0 copy-start
  7.2 0.0 all-reduce.2.cloned.1.call-start
  7.2 4.0 %fusion.36 = (bf16[120,1,1440]{2,1,0:T(2,128)(2,1)S(1)}, bf16[120,1,1440]{2,1,0:T(2,128)(2,1)S(1)}) fusion(bf16[120,8,1440]{2,1,0:T(8,128)(2,1)} %param.4), kind=kLoop, calls=%fused_computation.55 | loop fusion | bytes 1382400 | tf_op jit(solution)/shard_map/slice | solution.py:14
  11.2 0.8 copy.21
  12.0 3.1 %collective-permute-start = (bf16[120,1,1440]{2,0,1:T(8,128)(2,1)}, bf16[120,1,1440]{2,0,1:T(8,128)(2,1)}, u32[]{:S(2)}, u32[]{:S(2)}) collective-permute-start(bf16[120,1,1440]{2,0,1:T(8,128)(2,1)} %copy.21), channel_id=1, source_target_pairs={{0,1},{1,2},{2,3},{4,5},{5,6},{6,7},{8,9},{9,10},{10,11},{12,13},{... | collective-permute-start | bytes 1036808 | tf_op jit(solution)/shard_map/ppermute | solution.py:17
  15.2 0.8 copy.22
  16.0 1.3 collective-permute-start.1
  17.3 0.0 copy-done
  17.3 0.0 copy-start.3
  17.3 6.0 %fusion.35 = (f32[120,8,1439]{2,1,0:T(8,128)}, f32[120,8,1439]{2,1,0:T(8,128)}) fusion(bf16[120,8,1440]{2,1,0:T(8,128)(2,1)S(1)} %copy-done), kind=kLoop, calls=%fused_computation.54 | loop fusion | bytes 22103040 | tf_op jit(solution)/shard_map/jit(_roll_static)/slice | solution.py:46
  23.3 0.0 copy-start.1
  23.3 0.1 rsqrt_multiply_fusion
  24.2 0.0 copy-done.3
  24.2 0.9 fusion.34
  25.1 0.0 collective-permute-done
  25.1 1.6 copy.16
  26.7 0.0 collective-permute-done.1
  26.7 0.0 slice-start
  26.7 1.7 copy.17
  28.4 0.0 copy-done.1
  28.4 0.0 slice-start.1
  28.4 0.0 copy-start.2
  28.4 3.5 %convert_multiply_fusion = f32[120,10,1440]{2,1,0:T(8,128)S(1)} fusion(bf16[120,1,1440]{2,1,0:T(2,128)(2,1)S(1)} %copy.17, bf16[120,8,1440]{2,1,0:T(8,128)(2,1)S(1)} %copy-done.1, bf16[120,1,1440]{2,1,0:T(2,128)(2,1)S(1)} %copy.16, f32[10]{0:T(128)S(1)} %multiply_cosine_fusion), kind=kLoop, calls=%fused_computation.1 | loop fusion | flops 12096000 | bytes 10368040 | tf_op jit(solution)/shard_map/mul | solution.py:42
  31.9 0.0 slice-done
  31.9 0.0 slice-done.1
  32.0 0.0 copy-done.2
  32.0 6.7 %fusion.2 = bf16[120,8,1440]{2,1,0:T(8,128)(2,1)} fusion(f32[120,10,1440]{2,1,0:T(8,128)S(1)} %convert_multiply_fusion, f32[120,8,1]{2,1,0:T(8,128)S(1)} %copy-done.2, f32[120,8,1439]{2,1,0:T(8,128)} %get-tuple-element.5, f32[120,8,1439]{2,1,0:T(8,128)S(1)} %bitcast.19, f32[120,8,1]{2,1,0:T(8,128)S(1)} %get-tuple-element.2, f32[120]{0:T(128)S(1)} %compare_convert_fusion, ...), kind=kLoop, calls=%fused_computation.5 | loop fusion | flops 11059200 | bytes 24883712 | tf_op jit(solution)/shard_map/convert_element_type | solution.py:49
  38.6 5.6 %reshape.40 = bf16[120,11520]{1,0:T(8,128)(2,1)S(1)} reshape(bf16[120,8,1440]{2,1,0:T(8,128)(2,1)} %fusion.2) | data formatting | bytes 5529600 | tf_op jit(solution)/shard_map/reshape | solution.py:82
  44.3 1.7 fusion.14
  46.0 0.0 all-reduce.2.cloned.1.call-update
  46.0 90.7 %all-reduce.2.cloned.1.call-done = f32[32,11520]{1,0:T(8,128)} async-done(((f32[32,11520]{1,0:T(8,128)}), f32[32,11520]{1,0:T(8,128)}) %all-reduce.2.cloned.1.call-update) | async-done | bytes 1474576 | tf_op jit(solution)/shard_map/psum | solution.py:88
  136.7 3.2 %convolution_multiply_fusion.1 = f32[32,32]{0,1:T(8,128)S(1)} fusion(f32[32,11520]{1,0:T(8,128)} %all-reduce.2.cloned.1.call-done), kind=kOutput, calls=%fused_computation.9 | convolution fusion | flops 141558784 | bytes 1478656 | tf_op jit(solution)/shard_map/dot_general | solution.py:54
  139.8 11.2 %psum.22 = f32[32,32]{0,1:T(8,128)S(1)} all-reduce(f32[32,32]{0,1:T(8,128)S(1)} %convolution_multiply_fusion.1), channel_id=1, replica_groups=mesh['tm'=8,'lat'=4] {'lat'}, use_global_device_ids=true, to_apply=%region_1.2 | all-reduce | flops 1024 | bytes 8192 | tf_op jit(solution)/shard_map/psum | solution.py:89
  151.0 0.1 copy.19
  151.1 2.9 %cholesky.17 = f32[32,32]{1,0:T(8,128)S(1)} custom-call(f32[32,32]{1,0:T(8,128)S(1)} %fusion.13), custom_call_target="Cholesky" | custom-call | tf_op jit(solution)/shard_map/jit(cholesky)/cholesky | solution.py:66
  154.1 0.6 compare_reduce_fusion
  154.7 0.7 fusion.3
  155.4 2.4 %custom-call.6 = f32[1,32,32]{1,2,0:T(8,128)S(1)} custom-call(f32[1,32,32]{2,1,0:T(8,128)S(1)} %fusion.3), custom_call_target="InvertDiagBlocksLowerTriangular" | custom-call | tf_op jit(solution)/shard_map/triangular_solve | solution.py:67
  157.8 0.2 fusion.11
  158.0 2.7 %convolution_convert_fusion = bf16[32,11520]{1,0:T(8,128)(2,1)S(1)} fusion(f32[32,32]{1,0:T(8,128)S(1)} %fusion.11, f32[32,11520]{1,0:T(8,128)} %all-reduce.2.cloned.1.call-done), kind=kOutput, calls=%fused_computation | convolution fusion | flops 141926400 | bytes 2215936 | tf_op jit(solution)/shard_map/dot_general | solution.py:70
  160.8 0.9 convolution_multiply_fusion
  161.7 2.1 %reshape.41 = bf16[32,8,1440]{2,1,0:T(8,128)(2,1)} reshape(bf16[32,11520]{1,0:T(8,128)(2,1)S(1)} %convolution_convert_fusion) | data formatting | bytes 1474560 | tf_op jit(solution)/shard_map/reshape | solution.py:98
  163.8 10.9 %psum.23 = f32[32,120]{1,0:T(8,128)} all-reduce(f32[32,120]{1,0:T(8,128)S(1)} %convolution_multiply_fusion), channel_id=1, replica_groups=mesh['tm'=8,'lat'=4] {'lat'}, use_global_device_ids=true, to_apply=%region_4.5 | all-reduce | flops 3840 | bytes 30720 | tf_op jit(solution)/shard_map/psum | solution.py:97
  (7 shorter events, 0.1 us)
Async XLA Ops:
  7.2 10.1 %copy-start = (bf16[120,8,1440]{2,1,0:T(8,128)(2,1)S(1)}, bf16[120,8,1440]{2,1,0:T(8,128)(2,1)}, u32[]{:S(2)}) copy-start(bf16[120,8,1440]{2,1,0:T(8,128)(2,1)} %param.5) | copy-start | bytes 8294404
  7.2 129.5 %all-reduce.2.cloned.1.call-start = ((), (), s32[]{:S(2)}) async-start(), calls=%async_computation | async-start | bytes 2949120 | tf_op jit(solution)/shard_map/psum | solution.py:88
  12.0 13.1 %collective-permute-start = (bf16[120,1,1440]{2,0,1:T(8,128)(2,1)}, bf16[120,1,1440]{2,0,1:T(8,128)(2,1)}, u32[]{:S(2)}, u32[]{:S(2)}) collective-permute-start(bf16[120,1,1440]{2,0,1:T(8,128)(2,1)} %copy.21), channel_id=1, source_target_pairs={{0,1},{1,2},{2,3},{4,5},{5,6},{6,7},{8,9},{9,10},{10,11},{12,13},{... | collective-permute-start | bytes 1036808 | tf_op jit(solution)/shard_map/ppermute | solution.py:17
  16.0 10.7 %collective-permute-start.1 = (bf16[120,1,1440]{2,0,1:T(8,128)(2,1)}, bf16[120,1,1440]{2,0,1:T(8,128)(2,1)}, u32[]{:S(2)}, u32[]{:S(2)}) collective-permute-start(bf16[120,1,1440]{2,0,1:T(8,128)(2,1)} %copy.22), channel_id=1, source_target_pairs={{1,0},{2,1},{3,2},{5,4},{6,5},{7,6},{9,8},{10,9},{11,10},{13,12},{... | collective-permute-start | bytes 1036808 | tf_op jit(solution)/shard_map/ppermute | solution.py:19
  17.3 6.9 %copy-start.3 = (s32[120]{0:T(128)S(1)}, s32[120]{0:T(128)}, u32[]{:S(2)}) copy-start(s32[120]{0:T(128)} %param.7) | copy-start | bytes 1444
  23.3 5.1 %copy-start.1 = (bf16[120,8,1440]{2,1,0:T(8,128)(2,1)S(1)}, bf16[120,8,1440]{2,1,0:T(8,128)(2,1)}, u32[]{:S(2)}) copy-start(bf16[120,8,1440]{2,1,0:T(8,128)(2,1)} %param.4) | copy-start | bytes 8294404
  26.7 5.3 %slice-start = ((s8[5898240]{0:T(1024)(128)(4,1)}), s8[4194304]{0:T(1024)(128)(4,1)S(1)}, s32[]{:S(2)}) async-start(s8[5898240]{0:T(1024)(128)(4,1)} %bitcast.18), calls=%async_computation.1 | async-start | bytes 8388608
  28.4 3.5 %slice-start.1 = ((s8[5898240]{0:T(1024)(128)(4,1)}), s8[1703936]{0:T(1024)(128)(4,1)S(1)}, s32[]{:S(2)}) async-start(s8[5898240]{0:T(1024)(128)(4,1)} %bitcast.18), calls=%async_computation.2 | async-start | bytes 3407872
  28.4 3.5 %copy-start.2 = (f32[120,8,1]{2,1,0:T(8,128)S(1)}, f32[120,8,1]{2,1,0:T(8,128)}, u32[]{:S(2)}) copy-start(f32[120,8,1]{2,1,0:T(8,128)} %get-tuple-element.3) | copy-start | bytes 11524
Sparse Core Ops, SparseCore 0:
  46.1 90.5 all-reduce.1
where the time goes:
time: 182 us
  waiting for transfers between devices  90.7 us (50%)
  local copies, waits for them, and re-layouts  23.6 us (13%)
  blocking collectives  22 us (12%)
  other arithmetic  17 us (9%)
  between operations  15 us (8%)
  matrix products  8.73 us (5%)
  starting transfers between devices  4.44 us (2%)
    psum x1, waiting for transfers between devices, local(): sketch = lax.psum(sketch, 'tm')  90.7 us
    psum x1, blocking collectives, local(): gram_sum = lax.psum(local_gram(sketch, cell_total), 'lat')  11.2 us
    psum x1, blocking collectives, local(): coeffs = lax.psum(projected, 'lat')  10.9 us
    slice x2, local copies, waits for them, and re-layouts, metric_vorticity(): jnp.roll(meridional, 1, axis=2)  6.85 us
    convert_element_type x1, other arithmetic, metric_vorticity(): return field.astype(jnp.bfloat16)  6.66 us
    reshape x1, local copies, waits for them, and re-layouts, local(): metric_vorticity(padded_east, wind_north, padded_cosine, valid)  5.64 us
    slice x1, local copies, waits for them, and re-layouts, with_halo(): lax.slice_in_dim(cells, cells.shape[dim] - width, cells.shape[dim], axis=...  4.01 us
  transfers between devices with their start and end apart: 3, of which 1 were waited for; matrix products, arithmetic and copies ran while one was open for 5% of the time, Pallas kernels for 0%

commit v1 on v0

v1 whole, which is shorter than its diff:
```python
import functools

import jax
import jax.numpy as jnp
from jax import lax
from jax.experimental import pallas as pl
from jax.experimental.pallas import tpu as pltpu
from jax.sharding import PartitionSpec as P

RANK = 32
VMEM_LIMIT = 48 * 1024 * 1024
HIGHEST = lax.Precision.HIGHEST
WHOLE = pl.BlockSpec(memory_space=pltpu.VMEM)
SCALARS = pl.BlockSpec(memory_space=pltpu.SMEM)


def params():
    return pltpu.CompilerParams(vmem_limit_bytes=VMEM_LIMIT)


def mm(a, b, dims=((1,), (0,)), precision=None):
    return lax.dot_general(a, b, (dims, ((), ())), precision=precision, preferred_element_type=jnp.float32)


def iota(shape, axis):
    return lax.broadcasted_iota(jnp.int32, shape, axis)


def one_hot(condition):
    return condition.astype(jnp.float32).astype(jnp.bfloat16)


def pick_rows(value, rows, j):
    shape = (RANK, value.shape[0])
    return mm(one_hot(iota(shape, 1) == iota(shape, 0) * rows + j), value)


def padded_width(lon_count):
    return lon_count if lon_count % 128 == 0 else (lon_count + 2 + 127) // 128 * 128


def lon_shifts(value, lon_count):
    width = value.shape[1]
    return pltpu.roll(value, width - 1, 1), pltpu.roll(value, 1, 1)


def wrap_columns(ref, lon_count):
    width = ref.shape[1]
    if width != lon_count:
        ref[:, lon_count : lon_count + 1] = ref[:, 0:1]
        ref[:, width - 1 : width] = ref[:, lon_count - 1 : lon_count]


def sketch_kernel(
    rows, chunk, lon_count, scal_ref, ids_ref, coef_ref, east_ref, north_ref, main_ref, up_ref, down_ref,
    signs_ref, se_ref, sw_ref
):
    step = pl.program_id(0)
    slots = ids_ref.shape[1]
    per_piece = scal_ref[2]
    wide = RANK * rows

    @pl.when(step == 0)
    def _():
        order = iota((RANK, slots), 0)
        column = jnp.bitwise_xor(scal_ref[0], order // per_piece) * per_piece + order % per_piece
        mixed = ids_ref[...] * 1103515245 + column * 40503 + 12345
        mixed = jnp.bitwise_xor(mixed, jnp.right_shift(mixed, 13))
        mixed = mixed * 1664525 + 1013904223
        mixed = jnp.bitwise_xor(mixed, jnp.right_shift(mixed, 16))
        flipped = jnp.bitwise_and(jnp.right_shift(mixed, 7), 1)
        used = iota((RANK, slots), 1) < scal_ref[1]
        signs = jnp.where(used, 1 - 2 * flipped, 0).astype(jnp.float32).astype(jnp.bfloat16)
        spread = one_hot(iota((wide, RANK), 0) // rows == iota((wide, RANK), 1))
        tall = mm(spread, signs).astype(jnp.bfloat16)
        across = one_hot(iota((slots, slots * rows), 1) // rows == iota((slots, slots * rows), 0))
        full = mm(tall, across)
        same = iota(full.shape, 0) % rows == iota(full.shape, 1) % rows
        signs_ref[...] = jnp.where(same, full, 0.0).astype(jnp.bfloat16)

    place = pl.ds(pl.multiple_of(step * chunk, 128), chunk)
    se_ref[:, place] = mm(signs_ref[...], east_ref[...])
    sw_ref[:, place] = mm(signs_ref[...], north_ref[...])

    @pl.when(step == pl.num_programs(0) - 1)
    def _():
        wrap_columns(sw_ref, lon_count)
        rounded = se_ref[:, :lon_count].astype(jnp.bfloat16)
        up_ref[...] = pick_rows(rounded, rows, rows - 1).astype(jnp.bfloat16)
        down_ref[...] = pick_rows(rounded, rows, 0).astype(jnp.bfloat16)
        band = 4 * rows

        def body(index, carry):
            at = pl.ds(pl.multiple_of(index * band, band), band)
            ahead, behind = lon_shifts(sw_ref[at, : padded_width(lon_count)], lon_count)
            east = se_ref[at, : padded_width(lon_count)]
            north_side = pltpu.roll(east, 1, 0)
            south_side = pltpu.roll(east, band - 1, 0)
            total = (
                (ahead - behind) * coef_ref[at, 0:1]
                + north_side * coef_ref[at, 1:2]
                + south_side * coef_ref[at, 2:3]
            )
            main_ref[at, :] = total[:, :lon_count]
            return carry

        lax.fori_loop(0, RANK * rows // band, body, 0)


def halo_kernel(rows, scal_ref, coef_ref, main_ref, up_ref, down_ref, send_ref, keep_ref):
    per_piece = scal_ref[2]
    wide = RANK * rows
    half = wide // 2

    def real(order, me):
        return jnp.bitwise_xor(me, order // per_piece) * per_piece + order % per_piece

    row = iota((wide, RANK), 0)
    mine = real(row // rows, scal_ref[0])
    north_place = one_hot((mine == real(iota((wide, RANK), 1), scal_ref[3])) & (row % rows == 0))
    south_place = one_hot((mine == real(iota((wide, RANK), 1), scal_ref[3])) & (row % rows == rows - 1))
    total = main_ref[...] + coef_ref[:, 3:4] * (mm(north_place, up_ref[...]) + mm(south_place, down_ref[...]))
    keep_ref[...] = total[:half]
    send_ref[...] = total[half:].astype(jnp.bfloat16)


def project_kernel(
    rows, lon_count, piece_count, scal_ref, coef_ref, *refs
):
    piece_refs = refs[:piece_count]
    (up_ref, down_ref, east_ref, north_ref, sketch_ref, sums_ref, work, to_east, to_north, slots_ref) = refs[piece_count:]
    step = pl.program_id(0)
    wide = RANK * rows
    per_piece = scal_ref[2]
    piece_rows = RANK * rows // scal_static(piece_refs)
    fold = one_hot(iota((RANK, wide), 1) // rows == iota((RANK, wide), 0))

    @pl.when(step == 0)
    def _():
        start = 0
        for ref in piece_refs:
            for inner in range(ref.shape[0] // piece_rows):
                owner = jnp.bitwise_xor(scal_ref[0], start)
                at = pl.ds(pl.multiple_of(owner * piece_rows, piece_rows), piece_rows)
                sketch_ref[at, :] = ref[inner * piece_rows : (inner + 1) * piece_rows, :]
                start += 1
        work[:, :lon_count] = sketch_ref[...].astype(jnp.float32)
        wrap_columns(work, lon_count)
        band = 4 * rows

        def body(index, carry):
            at = pl.ds(pl.multiple_of(index * band, band), band)
            value = work[at, :]
            ahead, behind = lon_shifts(value, lon_count)
            to_north[at, :] = ((behind - ahead) * coef_ref[at, 0:1])[:, :lon_count].astype(jnp.bfloat16)
            above = pltpu.roll(value, 1, 0)
            below = pltpu.roll(value, band - 1, 0)
            to_east[at, :] = (above * coef_ref[at, 4:5] + below * coef_ref[at, 5:6])[:, :lon_count].astype(jnp.bfloat16)
            return carry

        lax.fori_loop(0, RANK * rows // band, body, 0)

    both = mm(east_ref[...], to_east[...], ((1,), (1,))) + mm(north_ref[...], to_north[...], ((1,), (1,)))
    same = iota(both.shape, 0) % rows == iota(both.shape, 1) % rows
    slots = both.shape[0] // rows
    summed = jnp.sum(jnp.where(same, both, 0.0).reshape(slots, rows, wide), axis=1)
    slots_ref[pl.ds(pl.multiple_of(step * slots, slots), slots), :] = summed

    @pl.when(step == pl.num_programs(0) - 1)
    def _():
        value = sketch_ref[...]
        gram = mm(value, value, ((1,), (1,)))
        same = iota(gram.shape, 0) % rows == iota(gram.shape, 1) % rows
        gram = jnp.sum(jnp.where(same, gram, 0.0).reshape(RANK, rows, wide), axis=1)
        gram = mm(gram, fold.astype(jnp.float32), ((1,), (1,)), HIGHEST)
        terms = mm(fold.astype(jnp.float32), slots_ref[...], ((1,), (1,)), HIGHEST)
        first = pick_rows(value, rows, 0)
        last = pick_rows(value, rows, rows - 1)
        first = (first * coef_ref[0:1, 3:4]).astype(jnp.bfloat16)
        last = (last * coef_ref[rows - 1 : rows, 3:4]).astype(jnp.bfloat16)
        terms += mm(first, up_ref[...], ((1,), (1,))) + mm(last, down_ref[...], ((1,), (1,)))
        width = terms.shape[1]
        sums_ref[...] = jnp.zeros_like(sums_ref)
        sums_ref[:, :width] = terms
        sums_ref[:, sums_ref.shape[1] - 128 : sums_ref.shape[1] - 128 + RANK] = gram


def scal_static(piece_refs):
    return sum(ref.shape[0] for ref in piece_refs) // piece_refs[0].shape[0]


def solve_kernel(rows, cell_total, scal_ref, sums_ref, sketch_ref, basis_ref, coeffs_ref, work):
    scale = 1.0 / cell_total
    slots = coeffs_ref.shape[1]
    wide = RANK * rows
    offset = sums_ref.shape[1] - 128
    work[...] = jnp.zeros_like(work)
    gram = sums_ref[:, offset : offset + RANK] * scale
    row, column = iota((RANK, RANK), 0), iota((RANK, RANK), 1)
    work[:, :RANK] = gram
    work[:, RANK : 2 * RANK] = (row == column).astype(jnp.float32)
    table = work[...]
    down, along = iota(table.shape, 0), iota(table.shape, 1)
    for k in range(RANK):
        pivot_row = table[k : k + 1, :]
        pivot = table[k : k + 1, k : k + 1]
        factor = jnp.where(down[:, 0:1] > k, table[:, k : k + 1] / pivot, 0.0)
        table = table - factor * pivot_row
    diagonal = jnp.sum(jnp.where(down == along, table, 0.0), axis=1, keepdims=True)
    work[...] = table * (1.0 / jnp.sqrt(diagonal))
    inverse = work[:, RANK : 2 * RANK]
    raw = mm(inverse, sums_ref[:, :slots], precision=HIGHEST) * scale
    coeffs_ref[...] = jnp.where(iota(raw.shape, 1) < scal_ref[1], raw, 0.0)
    spread = (iota((wide, RANK), 0) // rows == iota((wide, RANK), 1)).astype(jnp.float32)
    tall = mm(spread, inverse, precision=HIGHEST)
    large = mm(tall, spread, ((1,), (1,)), HIGHEST)
    same = iota(large.shape, 0) % rows == iota(large.shape, 1) % rows
    large = jnp.where(same, large, 0.0)
    high = large.astype(jnp.bfloat16)
    rest = large - high.astype(jnp.float32)
    middle = rest.astype(jnp.bfloat16)
    low = (rest - middle.astype(jnp.float32)).astype(jnp.bfloat16)
    value = sketch_ref[...]
    basis_ref[...] = (mm(high, value) + (mm(middle, value) + mm(low, value))).astype(jnp.bfloat16)


def cosine(row_index, total_rows):
    return jnp.cos((total_rows // 2 - row_index).astype(jnp.float32) * (jnp.pi / 720.0))


def coefficients(first_row, rows, total_rows):
    j = jnp.arange(rows, dtype=jnp.int32)
    here = first_row + j
    def weight(row):
        return 0.5 / jnp.sqrt(cosine(row, total_rows))
    first, last = j == 0, j == rows - 1
    north = -cosine(here - 1, total_rows) * weight(here)
    south = cosine(here + 1, total_rows) * weight(here)
    columns = [
        weight(here),
        jnp.where(first, 0.0, north),
        jnp.where(last, 0.0, south),
        jnp.where(first, north, jnp.where(last, south, 0.0)),
        jnp.where(first, 0.0, cosine(here, total_rows) * weight(here - 1)),
        jnp.where(last, 0.0, -cosine(here, total_rows) * weight(here + 1)),
    ]
    table = jnp.stack(columns + [jnp.zeros_like(columns[0])] * 2, axis=1)
    return jnp.tile(table, (RANK, 1))


def bit_order(lat, bits):
    order = list(range(bits))
    if lat % 2 and bits > 1:
        order[0], order[1] = order[1], order[0]
    return order


def relative_place(tm, parity, bits):
    def place(order):
        total = 0
        for turn, bit in enumerate(order):
            total = total + (((tm >> bit) & 1) << (bits - 1 - turn))
        return total
    return jnp.where(parity == 1, place(bit_order(1, bits)), place(bit_order(0, bits)))


def partners(turn, bits, tm_count, lat_count):
    pairs = []
    for tm in range(tm_count):
        for lat in range(lat_count):
            bit = bit_order(lat, bits)[turn]
            pairs.append((tm * lat_count + lat, (tm ^ (1 << bit)) * lat_count + lat))
    return pairs


def local(wind_east, wind_north, snap_counts, snap_ids):
    slots, rows, lon_count = wind_east.shape
    tm_count, lat_count = lax.axis_size("tm"), lax.axis_size("lat")
    bits = tm_count.bit_length() - 1
    tm, lat = lax.axis_index("tm"), lax.axis_index("lat")
    wide = RANK * rows
    per_piece = RANK // tm_count
    total_rows = rows * lat_count
    cell_total = total_rows * lon_count
    width = padded_width(lon_count)
    me = relative_place(tm, lat % 2, bits)
    beside = relative_place(tm, 1 - lat % 2, bits)
    scal = jnp.stack([me, snap_counts[0], jnp.int32(per_piece), beside]).astype(jnp.int32)
    coef = coefficients(lat * rows, rows, total_rows)
    east = wind_east.reshape(slots * rows, lon_count)
    north = wind_north.reshape(slots * rows, lon_count)
    northward = [(i + 1, i) for i in range(lat_count - 1)]
    southward = [(i, i + 1) for i in range(lat_count - 1)]

    chunk = 128 * -(-width // 512)
    steps = -(-width // chunk)
    field_spec = pl.BlockSpec((slots * rows, chunk), lambda i: (0, i))
    fixed = lambda shape: pl.BlockSpec(shape, lambda i: (0,) * len(shape))
    main, up, down = pl.pallas_call(
        functools.partial(sketch_kernel, rows, chunk, lon_count),
        grid=(steps,),
        in_specs=[SCALARS, fixed((1, slots)), fixed((wide, 8)), field_spec, field_spec],
        out_specs=[fixed((wide, lon_count)), fixed((RANK, lon_count)), fixed((RANK, lon_count))],
        out_shape=[
            jax.ShapeDtypeStruct((wide, lon_count), jnp.float32),
            jax.ShapeDtypeStruct((RANK, lon_count), jnp.bfloat16),
            jax.ShapeDtypeStruct((RANK, lon_count), jnp.bfloat16),
        ],
        scratch_shapes=[
            pltpu.VMEM((wide, slots * rows), jnp.bfloat16),
            pltpu.VMEM((wide, steps * chunk), jnp.float32),
            pltpu.VMEM((wide, steps * chunk), jnp.float32),
        ],
        compiler_params=params(),
        name="sketch_terms",
    )(scal, snap_ids.reshape(1, slots), coef, east, north)

    above = lax.ppermute(up, "lat", southward)
    below = lax.ppermute(down, "lat", northward)
    send, keep = pl.pallas_call(
        functools.partial(halo_kernel, rows),
        in_specs=[SCALARS] + [WHOLE] * 4,
        out_specs=[WHOLE, WHOLE],
        out_shape=[
            jax.ShapeDtypeStruct((wide // 2, lon_count), jnp.bfloat16),
            jax.ShapeDtypeStruct((wide // 2, lon_count), jnp.float32),
        ],
        compiler_params=params(),
        name="halo_terms",
    )(scal, coef, main, above, below)

    wind_above = lax.ppermute(wind_east[:, rows - 1, :], "lat", southward)
    wind_below = lax.ppermute(wind_east[:, 0, :], "lat", northward)

    both = ("tm", "lat")
    for turn in range(bits):
        got = lax.ppermute(send, both, partners(turn, bits, tm_count, lat_count))
        keep = keep + got.astype(jnp.float32)
        if turn < bits - 1:
            half = keep.shape[0] // 2
            send, keep = keep[half:].astype(jnp.bfloat16), keep[:half]
    held = keep.astype(jnp.bfloat16)
    pieces = [held]
    for turn in reversed(range(bits)):
        got = lax.ppermute(held, both, partners(turn, bits, tm_count, lat_count))
        pieces.append(got)
        if turn:
            held = jnp.concatenate([held, got], axis=0)

    slot_chunk = max(n for n in range(8, 33, 8) if slots % n == 0) if slots % 8 == 0 else slots
    slot_steps = slots // slot_chunk
    sums_width = -(-slots // 128) * 128 + 128
    row_spec = pl.BlockSpec((slot_chunk * rows, lon_count), lambda i: (i, 0))
    sketch, sums = pl.pallas_call(
        functools.partial(project_kernel, rows, lon_count, len(pieces)),
        grid=(slot_steps,),
        in_specs=[SCALARS, fixed((wide, 8))]
        + [fixed(piece.shape) for piece in pieces]
        + [fixed((slots, lon_count))] * 2
        + [row_spec, row_spec],
        out_specs=[fixed((wide, lon_count)), fixed((RANK, sums_width))],
        out_shape=[
            jax.ShapeDtypeStruct((wide, lon_count), jnp.bfloat16),
            jax.ShapeDtypeStruct((RANK, sums_width), jnp.float32),
        ],
        scratch_shapes=[
            pltpu.VMEM((wide, width), jnp.float32),
            pltpu.VMEM((wide, lon_count), jnp.bfloat16),
            pltpu.VMEM((wide, lon_count), jnp.bfloat16),
            pltpu.VMEM((slots, wide), jnp.float32),
        ],
        compiler_params=params(),
        name="projection_terms",
    )(scal, coef, *pieces, wind_above, wind_below, east, north)

    shift = 1
    while shift < lat_count:
        sums = sums + lax.ppermute(sums, "lat", [(i, i ^ shift) for i in range(lat_count)])
        shift *= 2

    basis, coeffs = pl.pallas_call(
        functools.partial(solve_kernel, rows, cell_total),
        in_specs=[SCALARS, WHOLE, WHOLE],
        out_specs=[WHOLE, WHOLE],
        out_shape=[
            jax.ShapeDtypeStruct((wide, lon_count), jnp.bfloat16),
            jax.ShapeDtypeStruct((RANK, slots), jnp.float32),
        ],
        scratch_shapes=[pltpu.VMEM((RANK, 128), jnp.float32)],
        compiler_params=params(),
        name="basis_and_coeffs",
    )(scal, sums, sketch)
    return basis.reshape(RANK, rows, lon_count), coeffs


def solution(mesh):
    in_specs = (P("tm", "lat", None), P("tm", "lat", None), P("tm"), P("tm"))
    out_specs = (P(None, "lat", None), P(None, "tm"))
    return jax.shard_map(local, mesh=mesh, in_specs=in_specs, out_specs=out_specs, check_vma=False)
```

time: 182 us -> 95.4 us (0.52)
  waiting for transfers between devices: 90.7 us -> 43.4 us
  Pallas kernels: 0 us -> 25.8 us
  blocking collectives: 22 us -> 0 us
  local copies, waits for them, and re-layouts: 23.6 us -> 3.68 us
  other arithmetic: 17 us -> 0.46 us
  starting transfers between devices: 4.44 us -> 20.2 us
  between operations: 15 us -> 1.5 us
  matrix products: 8.73 us -> 0 us
    psum x1 -> x0, waiting for transfers between devices: 90.7 us -> none  [local(): sketch = lax.psum(sketch, 'tm')]
    ppermute x2 -> x12, waiting for transfers between devices: 0.01 us -> 43.4 us  [the longest x3 16.4 us: local(): got = lax.ppermute(send, both, partners(turn, bits, tm_count, lat_count))]
    pallas_call x0 -> x4, Pallas kernels: none -> 25.8 us  [the longest x1 8.67 us: local(): pl.pallas_call(functools.partial(project_kernel, rows, lon_count, len(pie...]
    psum x2 -> x0, blocking collectives: 22 us -> none  [the longest x1 11.2 us: local(): gram_sum = lax.psum(local_gram(sketch, cell_total), 'lat')]
    ppermute x2 -> x12, starting transfers between devices: 4.4 us -> 20.2 us  [the longest x2 5.85 us: local(): lax.ppermute(sums, 'lat', [(i, i ^ shift) for i in range(lat_count)])]
    slice x3, local copies, waits for them, and re-layouts: 10.9 us -> 0.99 us  [the longest x1 0.95 us: local(): wind_below = lax.ppermute(wind_east[:, 0, :], 'lat', northward)]
    dot_general x4 -> x0, matrix products: 8.51 us -> none  [the longest x1 3.17 us: local_gram(): lax.dot_general(sketch, sketch, (((1,), (1,)), ((), ())), precision=lax.P...]
    reshape x2 -> x0, local copies, waits for them, and re-layouts: 7.77 us -> none  [the longest x1 5.64 us: local(): metric_vorticity(padded_east, wind_north, padded_cosine, valid)]
  transfers between devices with their start and end apart: 3 -> 12, of which waited for: 1 -> 9; matrix products, arithmetic and copies ran while one was open for 5% -> 1% of each run, Pallas kernels for 0% -> 0%
where the time goes in v1:
time: 95.4 us; the launch traced here: 95 us
  waiting for transfers between devices  43.4 us (45%)
  Pallas kernels  25.8 us (27%)
  starting transfers between devices  20.2 us (21%)
  local copies, waits for them, and re-layouts  3.68 us (4%)
  between operations  1.5 us (2%)
    ppermute x3, waiting for transfers between devices, local(): got = lax.ppermute(send, both, partners(turn, bits, tm_count, lat_count))  16.4 us
    ppermute x3, waiting for transfers between devices, local(): got = lax.ppermute(held, both, partners(turn, bits, tm_count, lat_count))  12.9 us
    pallas_call x1, Pallas kernels, local(): pl.pallas_call(functools.partial(project_kernel, rows, lon_count, len(pie...  8.67 us
    pallas_call x1, Pallas kernels, local(): pl.pallas_call(functools.partial(sketch_kernel, rows, chunk, lon_count),...  7.6 us
    pallas_call x1, Pallas kernels, local(): pl.pallas_call(functools.partial(solve_kernel, rows, cell_total), in_spec...  5.87 us
    ppermute x2, starting transfers between devices, local(): lax.ppermute(sums, 'lat', [(i, i ^ shift) for i in range(lat_count)])  5.85 us
    ppermute x3, starting transfers between devices, local(): got = lax.ppermute(send, both, partners(turn, bits, tm_count, lat_count))  5.84 us
    ppermute x1, waiting for transfers between devices, local(): wind_below = lax.ppermute(wind_east[:, 0, :], 'lat', northward)  5.4 us
  transfers between devices with their start and end apart: 12, of which 9 were waited for; matrix products, arithmetic and copies ran while one was open for 1% of the time, Pallas kernels for 0%

profile of v1, /device:TPU:0, one launch (start us, length us, event | category | flops | bytes accessed | tf_op | source)
XLA Modules:
  0.0 95.0 jit_solution(1573308799038090635)
XLA Ops:
  0.7 0.1 multiply_select_fusion
  0.7 0.1 select_select_fusion
  0.8 0.1 fusion.2
  1.5 0.1 stack.21
  1.6 0.1 pad_add_fusion.scal_ref
  1.7 0.0 copy-start
  1.7 1.8 %copy-done = bf16[120,8,1440]{2,1,0:T(8,128)(2,1)S(1)} copy-done((bf16[120,8,1440]{2,1,0:T(8,128)(2,1)S(1)}, bf16[120,8,1440]{2,1,0:T(8,128)(2,1)}, u32[]{:S(2)}) %copy-start) | copy-done | bytes 2764824
  3.6 0.0 copy-start.2
  3.6 0.7 copy-done.2
  4.2 7.6 %sketch_terms.1 = (f32[256,1440]{1,0:T(8,128)S(1)}, bf16[32,1440]{1,0:T(8,128)(2,1)S(1)}, bf16[32,1440]{1,0:T(8,128)(2,1)S(1)}) custom-call(s32[4]{0:T(128)S(1)} %pad_add_fusion.scal_ref, s32[1,120]{1,0:T(1,128)S(1)} %bitcast.16, f32[256,8]{1,0:T(8,128)S(1)} %broadcast_bitcast_fusion.coef_ref, bf16[960,1440]{1,0:T(8,128)(2,1)S(1)} %bitcast.14, ...), custom_call_target="tpu_custom_call" | custom-call | tf_op jit(solution)/shard_map/sketch_terms/pallas_call | solution.py:299
  11.8 2.4 %collective-permute-start = (bf16[32,1440]{1,0:T(8,128)(2,1)S(1)}, bf16[32,1440]{1,0:T(8,128)(2,1)S(1)}, u32[]{:S(2)}, u32[]{:S(2)}) collective-permute-start(bf16[32,1440]{1,0:T(8,128)(2,1)S(1)} %get-tuple-element.12), channel_id=1, source_target_pairs={{0,1},{1,2},{2,3},{4,5},{5,6},{6,7},{8,9},{9,10},{10,11},{12,13},{... | collective-permute-start | bytes 276488 | tf_op jit(solution)/shard_map/ppermute | solution.py:318
  14.2 1.3 %collective-permute-start.1 = (bf16[32,1440]{1,0:T(8,128)(2,1)S(1)}, bf16[32,1440]{1,0:T(8,128)(2,1)S(1)}, u32[]{:S(2)}, u32[]{:S(2)}) collective-permute-start(bf16[32,1440]{1,0:T(8,128)(2,1)S(1)} %get-tuple-element.13), channel_id=1, source_target_pairs={{1,0},{2,1},{3,2},{5,4},{6,5},{7,6},{9,8},{10,9},{11,10},{13,12},{... | collective-permute-start | bytes 276488 | tf_op jit(solution)/shard_map/ppermute | solution.py:319
  15.5 0.0 collective-permute-done.up_ref
  15.5 4.0 %collective-permute-done.1.down_ref = bf16[32,1440]{1,0:T(8,128)(2,1)S(1)} collective-permute-done((bf16[32,1440]{1,0:T(8,128)(2,1)S(1)}, bf16[32,1440]{1,0:T(8,128)(2,1)S(1)}, u32[]{:S(2)}, u32[]{:S(2)}) %collective-permute-start.1) | collective-permute-done | bytes 92192 | tf_op jit(solution)/shard_map/ppermute | solution.py:319
  19.5 3.6 %halo_terms.1 = (bf16[128,1440]{1,0:T(8,128)(2,1)S(1)}, f32[128,1440]{1,0:T(8,128)S(1)}) custom-call(s32[4]{0:T(128)S(1)} %pad_add_fusion.scal_ref, f32[256,8]{1,0:T(8,128)S(1)} %broadcast_bitcast_fusion.coef_ref, f32[256,1440]{1,0:T(8,128)S(1)} %get-tuple-element.11.main_ref, bf16[32,1440]{1,0:T(8,128)(2,1)S(1)} %collective-permute-done.up_ref, ...), custom_call_target="tpu_custom_call" | custom-call | tf_op jit(solution)/shard_map/halo_terms/pallas_call | solution.py:320
  23.1 0.0 copy-start.1
  23.2 1.6 %collective-permute-start.2 = (bf16[128,1440]{1,0:T(8,128)(2,1)S(1)}, bf16[128,1440]{1,0:T(8,128)(2,1)S(1)}, u32[]{:S(2)}, u32[]{:S(2)}) collective-permute-start(bf16[128,1440]{1,0:T(8,128)(2,1)S(1)} %get-tuple-element.15), channel_id=1, source_target_pairs={{0,4},{1,9},{2,6},{3,11},{4,0},{5,13},{6,2},{7,15},{8,12},{9,1},{1... | collective-permute-start | bytes 1105928 | tf_op jit(solution)/shard_map/ppermute | solution.py:337
  24.7 6.3 %collective-permute-done.2 = bf16[128,1440]{1,0:T(8,128)(2,1)S(1)} collective-permute-done((bf16[128,1440]{1,0:T(8,128)(2,1)S(1)}, bf16[128,1440]{1,0:T(8,128)(2,1)S(1)}, u32[]{:S(2)}, u32[]{:S(2)}) %collective-permute-start.2) | collective-permute-done | bytes 368672 | tf_op jit(solution)/shard_map/ppermute | solution.py:337
  31.0 0.1 convert_add_fusion
  31.1 1.6 %collective-permute-start.3 = (bf16[64,1440]{1,0:T(8,128)(2,1)S(1)}, bf16[64,1440]{1,0:T(8,128)(2,1)S(1)}, u32[]{:S(2)}, u32[]{:S(2)}) collective-permute-start(bf16[64,1440]{1,0:T(8,128)(2,1)S(1)} %slice.36), channel_id=1, source_target_pairs={{0,8},{1,5},{2,10},{3,7},{4,12},{5,1},{6,14},{7,3},{8,0},{9,13},{1... | collective-permute-start | bytes 552968 | tf_op jit(solution)/shard_map/ppermute | solution.py:337
  32.7 4.1 %collective-permute-done.3 = bf16[64,1440]{1,0:T(8,128)(2,1)S(1)} collective-permute-done((bf16[64,1440]{1,0:T(8,128)(2,1)S(1)}, bf16[64,1440]{1,0:T(8,128)(2,1)S(1)}, u32[]{:S(2)}, u32[]{:S(2)}) %collective-permute-start.3) | collective-permute-done | bytes 184352 | tf_op jit(solution)/shard_map/ppermute | solution.py:337
  36.9 2.6 %collective-permute-start.4 = (bf16[32,1440]{1,0:T(8,128)(2,1)S(1)}, bf16[32,1440]{1,0:T(8,128)(2,1)S(1)}, u32[]{:S(2)}, u32[]{:S(2)}) collective-permute-start(bf16[32,1440]{1,0:T(8,128)(2,1)S(1)} %slice.37), channel_id=1, source_target_pairs={{0,16},{1,17},{2,18},{3,19},{4,20},{5,21},{6,22},{7,23},{8,24},{9,... | collective-permute-start | bytes 276488 | tf_op jit(solution)/shard_map/ppermute | solution.py:337
  39.5 6.1 %collective-permute-done.4 = bf16[32,1440]{1,0:T(8,128)(2,1)S(1)} collective-permute-done((bf16[32,1440]{1,0:T(8,128)(2,1)S(1)}, bf16[32,1440]{1,0:T(8,128)(2,1)S(1)}, u32[]{:S(2)}, u32[]{:S(2)}) %collective-permute-start.4) | collective-permute-done | bytes 92192 | tf_op jit(solution)/shard_map/ppermute | solution.py:337
  45.6 0.6 collective-permute-start.5
  46.3 7.2 %collective-permute-done.5.refs_1_ = bf16[32,1440]{1,0:T(8,128)(2,1)S(1)} collective-permute-done((bf16[32,1440]{1,0:T(8,128)(2,1)S(1)}, bf16[32,1440]{1,0:T(8,128)(2,1)S(1)}, u32[]{:S(2)}, u32[]{:S(2)}) %collective-permute-start.5) | collective-permute-done | bytes 92192 | tf_op jit(solution)/shard_map/ppermute | solution.py:345
  53.5 0.1 collective-permute-start.6
  53.6 5.7 %collective-permute-done.6.refs_2_ = bf16[64,1440]{1,0:T(8,128)(2,1)S(1)} collective-permute-done((bf16[64,1440]{1,0:T(8,128)(2,1)S(1)}, bf16[64,1440]{1,0:T(8,128)(2,1)S(1)}, u32[]{:S(2)}, u32[]{:S(2)}) %collective-permute-start.6) | collective-permute-done | bytes 184352 | tf_op jit(solution)/shard_map/ppermute | solution.py:345
  59.3 1.6 %collective-permute-start.7 = (bf16[128,1440]{1,0:T(8,128)(2,1)S(1)}, bf16[128,1440]{1,0:T(8,128)(2,1)S(1)}, u32[]{:S(2)}, u32[]{:S(2)}) collective-permute-start(bf16[128,1440]{1,0:T(8,128)(2,1)S(1)} %pad_maximum_fusion), channel_id=1, source_target_pairs={{0,4},{1,9},{2,6},{3,11},{4,0},{5,13},{6,2},{7,15},{8,12},{9,1},{1... | collective-permute-start | bytes 1105928 | tf_op jit(solution)/shard_map/ppermute | solution.py:345
  60.8 0.0 copy-done.1
  60.8 1.0 %fusion.4 = (bf16[120,1,1440]{2,1,0:T(2,128)(2,1)S(1)}, bf16[120,1,1440]{2,1,0:T(2,128)(2,1)S(1)}) fusion(bf16[120,8,1440]{2,1,0:T(8,128)(2,1)S(1)} %copy-done.1), kind=kLoop, calls=%fused_computation.26 | loop fusion | bytes 1382400 | tf_op jit(solution)/shard_map/slice | solution.py:333
  61.8 0.1 copy.13
  61.9 1.3 %collective-permute-start.8 = (bf16[120,1440]{1,0:T(8,128)(2,1)S(1)}, bf16[120,1440]{1,0:T(8,128)(2,1)S(1)}, u32[]{:S(2)}, u32[]{:S(2)}) collective-permute-start(bf16[120,1440]{1,0:T(8,128)(2,1)S(1)} %bitcast.19), channel_id=1, source_target_pairs={{0,1},{1,2},{2,3},{4,5},{5,6},{6,7},{8,9},{9,10},{10,11},{12,13},{... | collective-permute-start | bytes 1036808 | tf_op jit(solution)/shard_map/ppermute | solution.py:332
  63.2 0.1 copy.12
  63.2 1.3 %collective-permute-start.9 = (bf16[120,1440]{1,0:T(8,128)(2,1)S(1)}, bf16[120,1440]{1,0:T(8,128)(2,1)S(1)}, u32[]{:S(2)}, u32[]{:S(2)}) collective-permute-start(bf16[120,1440]{1,0:T(8,128)(2,1)S(1)} %bitcast.20), channel_id=1, source_target_pairs={{1,0},{2,1},{3,2},{5,4},{6,5},{7,6},{9,8},{10,9},{11,10},{13,12},{... | collective-permute-start | bytes 1036808 | tf_op jit(solution)/shard_map/ppermute | solution.py:333
  64.5 0.0 collective-permute-done.8.refs_4_
  64.5 5.4 %collective-permute-done.9.refs_5_ = bf16[120,1440]{1,0:T(8,128)(2,1)S(1)} collective-permute-done((bf16[120,1440]{1,0:T(8,128)(2,1)S(1)}, bf16[120,1440]{1,0:T(8,128)(2,1)S(1)}, u32[]{:S(2)}, u32[]{:S(2)}) %collective-permute-start.9) | collective-permute-done | bytes 345632 | tf_op jit(solution)/shard_map/ppermute | solution.py:333
  69.9 0.0 collective-permute-done.7.refs_3_
  69.9 8.7 %projection_terms.1 = (bf16[256,1440]{1,0:T(8,128)(2,1)S(1)}, f32[32,256]{1,0:T(8,128)S(1)}) custom-call(s32[4]{0:T(128)S(1)} %pad_add_fusion.scal_ref, f32[256,8]{1,0:T(8,128)S(1)} %broadcast_bitcast_fusion.coef_ref, bf16[32,1440]{1,0:T(8,128)(2,1)S(1)} %fusion.refs_0_, bf16[32,1440]{1,0:T(8,128)(2,1)S(1)} %collective-permute-done.5.refs_1_, ...), custom_call_target="tpu_custom_call" | custom-call | tf_op jit(solution)/shard_map/projection_terms/pallas_call | solution.py:354
  78.6 5.8 %collective-permute-start.10 = (f32[32,256]{1,0:T(8,128)S(1)}, f32[32,256]{1,0:T(8,128)S(1)}, u32[]{:S(2)}, u32[]{:S(2)}) collective-permute-start(f32[32,256]{1,0:T(8,128)S(1)} %get-tuple-element.16), channel_id=1, source_target_pairs={{0,1},{1,0},{2,3},{3,2},{4,5},{5,4},{6,7},{7,6},{8,9},{9,8},{10,11... | collective-permute-start | bytes 98312 | tf_op jit(solution)/shard_map/ppermute | solution.py:378
  84.4 0.9 collective-permute-done.10
  85.2 0.1 collective-permute-start.11
  85.3 3.8 %collective-permute-done.11 = f32[32,256]{1,0:T(8,128)S(1)} collective-permute-done((f32[32,256]{1,0:T(8,128)S(1)}, f32[32,256]{1,0:T(8,128)S(1)}, u32[]{:S(2)}, u32[]{:S(2)}) %collective-permute-start.11) | collective-permute-done | bytes 32800 | tf_op jit(solution)/shard_map/ppermute | solution.py:378
  89.2 5.9 %basis_and_coeffs.1 = (bf16[256,1440]{1,0:T(8,128)(2,1)}, f32[32,120]{1,0:T(8,128)}) custom-call(s32[4]{0:T(128)S(1)} %pad_add_fusion.scal_ref, f32[32,256]{1,0:T(8,128)S(1)} %add.116.sums_ref, bf16[256,1440]{1,0:T(8,128)(2,1)S(1)} %get-tuple-element.17.sketch_ref), custom_call_target="tpu_custom_call" | custom-call | tf_op jit(solution)/shard_map/basis_and_coeffs/pallas_call | solution.py:381
  (10 shorter events, 0.2 us)
Async XLA Ops:
  1.7 1.8 %copy-start = (bf16[120,8,1440]{2,1,0:T(8,128)(2,1)S(1)}, bf16[120,8,1440]{2,1,0:T(8,128)(2,1)}, u32[]{:S(2)}) copy-start(bf16[120,8,1440]{2,1,0:T(8,128)(2,1)} %param.4) | copy-start | bytes 8294404
  3.6 0.7 copy-start.2
  11.8 3.7 %collective-permute-start = (bf16[32,1440]{1,0:T(8,128)(2,1)S(1)}, bf16[32,1440]{1,0:T(8,128)(2,1)S(1)}, u32[]{:S(2)}, u32[]{:S(2)}) collective-permute-start(bf16[32,1440]{1,0:T(8,128)(2,1)S(1)} %get-tuple-element.12), channel_id=1, source_target_pairs={{0,1},{1,2},{2,3},{4,5},{5,6},{6,7},{8,9},{9,10},{10,11},{12,13},{... | collective-permute-start | bytes 276488 | tf_op jit(solution)/shard_map/ppermute | solution.py:318
  14.2 5.3 %collective-permute-start.1 = (bf16[32,1440]{1,0:T(8,128)(2,1)S(1)}, bf16[32,1440]{1,0:T(8,128)(2,1)S(1)}, u32[]{:S(2)}, u32[]{:S(2)}) collective-permute-start(bf16[32,1440]{1,0:T(8,128)(2,1)S(1)} %get-tuple-element.13), channel_id=1, source_target_pairs={{1,0},{2,1},{3,2},{5,4},{6,5},{7,6},{9,8},{10,9},{11,10},{13,12},{... | collective-permute-start | bytes 276488 | tf_op jit(solution)/shard_map/ppermute | solution.py:319
  23.1 37.7 %copy-start.1 = (bf16[120,8,1440]{2,1,0:T(8,128)(2,1)S(1)}, bf16[120,8,1440]{2,1,0:T(8,128)(2,1)}, u32[]{:S(2)}) copy-start(bf16[120,8,1440]{2,1,0:T(8,128)(2,1)} %param.4) | copy-start | bytes 8294404
  23.2 7.8 %collective-permute-start.2 = (bf16[128,1440]{1,0:T(8,128)(2,1)S(1)}, bf16[128,1440]{1,0:T(8,128)(2,1)S(1)}, u32[]{:S(2)}, u32[]{:S(2)}) collective-permute-start(bf16[128,1440]{1,0:T(8,128)(2,1)S(1)} %get-tuple-element.15), channel_id=1, source_target_pairs={{0,4},{1,9},{2,6},{3,11},{4,0},{5,13},{6,2},{7,15},{8,12},{9,1},{1... | collective-permute-start | bytes 1105928 | tf_op jit(solution)/shard_map/ppermute | solution.py:337
  31.1 5.7 %collective-permute-start.3 = (bf16[64,1440]{1,0:T(8,128)(2,1)S(1)}, bf16[64,1440]{1,0:T(8,128)(2,1)S(1)}, u32[]{:S(2)}, u32[]{:S(2)}) collective-permute-start(bf16[64,1440]{1,0:T(8,128)(2,1)S(1)} %slice.36), channel_id=1, source_target_pairs={{0,8},{1,5},{2,10},{3,7},{4,12},{5,1},{6,14},{7,3},{8,0},{9,13},{1... | collective-permute-start | bytes 552968 | tf_op jit(solution)/shard_map/ppermute | solution.py:337
  36.9 8.7 %collective-permute-start.4 = (bf16[32,1440]{1,0:T(8,128)(2,1)S(1)}, bf16[32,1440]{1,0:T(8,128)(2,1)S(1)}, u32[]{:S(2)}, u32[]{:S(2)}) collective-permute-start(bf16[32,1440]{1,0:T(8,128)(2,1)S(1)} %slice.37), channel_id=1, source_target_pairs={{0,16},{1,17},{2,18},{3,19},{4,20},{5,21},{6,22},{7,23},{8,24},{9,... | collective-permute-start | bytes 276488 | tf_op jit(solution)/shard_map/ppermute | solution.py:337
  45.6 7.9 %collective-permute-start.5 = (bf16[32,1440]{1,0:T(8,128)(2,1)S(1)}, bf16[32,1440]{1,0:T(8,128)(2,1)S(1)}, u32[]{:S(2)}, u32[]{:S(2)}) collective-permute-start(bf16[32,1440]{1,0:T(8,128)(2,1)S(1)} %fusion.refs_0_), channel_id=1, source_target_pairs={{0,16},{1,17},{2,18},{3,19},{4,20},{5,21},{6,22},{7,23},{8,24},{9,... | collective-permute-start | bytes 276488 | tf_op jit(solution)/shard_map/ppermute | solution.py:345
  53.5 5.7 %collective-permute-start.6 = (bf16[64,1440]{1,0:T(8,128)(2,1)S(1)}, bf16[64,1440]{1,0:T(8,128)(2,1)S(1)}, u32[]{:S(2)}, u32[]{:S(2)}) collective-permute-start(bf16[64,1440]{1,0:T(8,128)(2,1)S(1)} %pad_maximum_fusion.1), channel_id=1, source_target_pairs={{0,8},{1,5},{2,10},{3,7},{4,12},{5,1},{6,14},{7,3},{8,0},{9,13},{1... | collective-permute-start | bytes 552968 | tf_op jit(solution)/shard_map/ppermute | solution.py:345
  59.3 10.7 %collective-permute-start.7 = (bf16[128,1440]{1,0:T(8,128)(2,1)S(1)}, bf16[128,1440]{1,0:T(8,128)(2,1)S(1)}, u32[]{:S(2)}, u32[]{:S(2)}) collective-permute-start(bf16[128,1440]{1,0:T(8,128)(2,1)S(1)} %pad_maximum_fusion), channel_id=1, source_target_pairs={{0,4},{1,9},{2,6},{3,11},{4,0},{5,13},{6,2},{7,15},{8,12},{9,1},{1... | collective-permute-start | bytes 1105928 | tf_op jit(solution)/shard_map/ppermute | solution.py:345
  61.9 2.7 %collective-permute-start.8 = (bf16[120,1440]{1,0:T(8,128)(2,1)S(1)}, bf16[120,1440]{1,0:T(8,128)(2,1)S(1)}, u32[]{:S(2)}, u32[]{:S(2)}) collective-permute-start(bf16[120,1440]{1,0:T(8,128)(2,1)S(1)} %bitcast.19), channel_id=1, source_target_pairs={{0,1},{1,2},{2,3},{4,5},{5,6},{6,7},{8,9},{9,10},{10,11},{12,13},{... | collective-permute-start | bytes 1036808 | tf_op jit(solution)/shard_map/ppermute | solution.py:332
  63.2 6.7 %collective-permute-start.9 = (bf16[120,1440]{1,0:T(8,128)(2,1)S(1)}, bf16[120,1440]{1,0:T(8,128)(2,1)S(1)}, u32[]{:S(2)}, u32[]{:S(2)}) collective-permute-start(bf16[120,1440]{1,0:T(8,128)(2,1)S(1)} %bitcast.20), channel_id=1, source_target_pairs={{1,0},{2,1},{3,2},{5,4},{6,5},{7,6},{9,8},{10,9},{11,10},{13,12},{... | collective-permute-start | bytes 1036808 | tf_op jit(solution)/shard_map/ppermute | solution.py:333
  78.6 6.6 %collective-permute-start.10 = (f32[32,256]{1,0:T(8,128)S(1)}, f32[32,256]{1,0:T(8,128)S(1)}, u32[]{:S(2)}, u32[]{:S(2)}) collective-permute-start(f32[32,256]{1,0:T(8,128)S(1)} %get-tuple-element.16), channel_id=1, source_target_pairs={{0,1},{1,0},{2,3},{3,2},{4,5},{5,4},{6,7},{7,6},{8,9},{9,8},{10,11... | collective-permute-start | bytes 98312 | tf_op jit(solution)/shard_map/ppermute | solution.py:378
  85.2 3.9 %collective-permute-start.11 = (f32[32,256]{1,0:T(8,128)S(1)}, f32[32,256]{1,0:T(8,128)S(1)}, u32[]{:S(2)}, u32[]{:S(2)}) collective-permute-start(f32[32,256]{1,0:T(8,128)S(1)} %add.115), channel_id=1, source_target_pairs={{0,2},{1,3},{2,0},{3,1},{4,6},{5,7},{6,4},{7,5},{8,10},{9,11},{10,... | collective-permute-start | bytes 98312 | tf_op jit(solution)/shard_map/ppermute | solution.py:378

commit v2 on v0

v2 whole, which is shorter than its diff:
```python
import functools

import jax
import jax.numpy as jnp
from jax import lax
from jax.experimental import pallas as pl
from jax.experimental.pallas import tpu as pltpu
from jax.sharding import PartitionSpec as P

RANK = 32
VMEM_LIMIT = 32 * 1024 * 1024
HIGHEST = lax.Precision.HIGHEST
WHOLE = pl.BlockSpec(memory_space=pltpu.VMEM)
SCALARS = pl.BlockSpec(memory_space=pltpu.SMEM)
FAR = pl.BlockSpec(memory_space=pltpu.HBM)


def in_hbm(array):
    return pltpu.with_memory_space_constraint(array, pltpu.HBM)


def params():
    return pltpu.CompilerParams(vmem_limit_bytes=VMEM_LIMIT)


def mm(a, b, dims=((1,), (0,)), precision=None):
    return lax.dot_general(a, b, (dims, ((), ())), precision=precision, preferred_element_type=jnp.float32)


def iota(shape, axis):
    return lax.broadcasted_iota(jnp.int32, shape, axis)


def one_hot(condition):
    return jnp.where(condition, 1.0, 0.0).astype(jnp.bfloat16)


def group(count, rows, axis):
    index = iota((count, 1) if axis == 0 else (1, count), axis)
    if rows & (rows - 1) == 0:
        return jnp.right_shift(index, rows.bit_length() - 1), jnp.bitwise_and(index, rows - 1)
    return index // rows, index % rows


def spread_rows(rows):
    return one_hot(group(RANK * rows, rows, 0)[0] == iota((1, RANK), 1))


def same_place(tall, wide, rows):
    return group(tall, rows, 0)[1] == group(wide, rows, 1)[1]


def pick_rows(value, rows, j):
    return mm(one_hot(iota((1, value.shape[0]), 1) == iota((RANK, 1), 0) * rows + j), value)


def padded_width(lon_count):
    return lon_count if lon_count % 128 == 0 else (lon_count + 2 + 127) // 128 * 128


def lon_shifts(value):
    return pltpu.roll(value, value.shape[1] - 1, 1), pltpu.roll(value, 1, 1)


def wrap_columns(ref, lon_count):
    width = ref.shape[1]
    if width != lon_count:
        ref[:, lon_count : lon_count + 1] = ref[:, 0:1]
        ref[:, width - 1 : width] = ref[:, lon_count - 1 : lon_count]


def bit_order(lat, bits):
    order = list(range(bits))
    if lat % 2 and bits > 1:
        order[0], order[1] = order[1], order[0]
    return order


def relative_place(tm, parity, bits):
    def place(order):
        total = 0
        for turn, bit in enumerate(order):
            total = total + (((tm >> bit) & 1) << (bits - 1 - turn))
        return total
    return jnp.where(parity == 1, place(bit_order(1, bits)), place(bit_order(0, bits)))


def places():
    bits = lax.axis_size("tm").bit_length() - 1
    tm, parity = lax.axis_index("tm"), jnp.bitwise_and(lax.axis_index("lat"), 1)
    return relative_place(tm, parity, bits), relative_place(tm, 1 - parity, bits)


def real_column(order, place):
    per_piece = RANK // lax.axis_size("tm")
    part, inner = group(RANK, per_piece, 0 if order.shape[1] == 1 else 1)
    if order.shape[0] * order.shape[1] != RANK:
        part, inner = order // per_piece, order % per_piece
    return jnp.bitwise_xor(part, place) * per_piece + inner


def geometry(rows, repeat):
    total_rows = rows * lax.axis_size("lat")
    j = group(rows * repeat, rows, 0)[1]
    here = lax.axis_index("lat") * rows + j

    def cosine(row):
        return jnp.cos((total_rows // 2 - row).astype(jnp.float32) * (jnp.pi / 720.0))

    return j, cosine(here - 1), cosine(here), cosine(here + 1)


def weight(cosines):
    return 0.5 / jnp.sqrt(cosines)


def east_kernel(rows, lon_count, count_ref, ids_hbm, east_hbm, part_ref, up_ref, down_ref, signs_ref, ids, east, se, sems):
    slots = ids.shape[1]
    wide = RANK * rows
    cut = slots * rows // 32 * 16
    head = pltpu.make_async_copy(east_hbm.at[pl.ds(0, cut)], east.at[pl.ds(0, cut)], sems.at[0])
    tail = pltpu.make_async_copy(
        east_hbm.at[pl.ds(cut, slots * rows - cut)], east.at[pl.ds(cut, slots * rows - cut)], sems.at[1]
    )
    keys = pltpu.make_async_copy(ids_hbm, ids, sems.at[2])
    keys.start()
    head.start()
    tail.start()
    me, _ = places()
    order = iota((RANK, 1), 0)
    column = real_column(order, me)
    spread = spread_rows(rows)
    across = one_hot(group(slots * rows, rows, 1)[0] == iota((slots, 1), 0))
    j, c_north, c_here, c_south = geometry(rows, 4)
    north = jnp.where(j == 0, 0.0, -c_north * weight(c_here))
    south = jnp.where(j == rows - 1, 0.0, c_south * weight(c_here))
    keys.wait()
    mixed = ids[...] * 1103515245 + (column * 40503 + 12345)
    mixed = jnp.bitwise_xor(mixed, jnp.right_shift(mixed, 13))
    mixed = mixed * 1664525 + 1013904223
    mixed = jnp.bitwise_xor(mixed, jnp.right_shift(mixed, 16))
    flipped = jnp.bitwise_and(jnp.right_shift(mixed, 7), 1)
    used = iota((1, slots), 1) < count_ref[0]
    signs = jnp.where(used, 1 - 2 * flipped, 0).astype(jnp.float32).astype(jnp.bfloat16)
    full = mm(mm(spread, signs).astype(jnp.bfloat16), across)
    signs_ref[...] = jnp.where(same_place(wide, slots * rows, rows), full, 0.0).astype(jnp.bfloat16)
    head.wait()
    se[:, :lon_count] = mm(signs_ref[:, :cut], east[:cut, :])
    tail.wait()
    se[:, :lon_count] += mm(signs_ref[:, cut:], east[cut:, :])
    rounded = se[:, :lon_count].astype(jnp.bfloat16)
    up_ref[...] = pick_rows(rounded, rows, rows - 1).astype(jnp.bfloat16)
    down_ref[...] = pick_rows(rounded, rows, 0).astype(jnp.bfloat16)
    band = 4 * rows

    def body(index, carry):
        at = pl.ds(pl.multiple_of(index * band, band), band)
        value = se[at, :lon_count]
        part_ref[at, :] = pltpu.roll(value, 1, 0) * north + pltpu.roll(value, band - 1, 0) * south
        return carry

    lax.fori_loop(0, wide // band, body, 0)


def north_kernel(rows, lon_count, signs_ref, part_ref, north_ref, main_ref, sw):
    sw[:, :lon_count] = mm(signs_ref[...], north_ref[...])
    wrap_columns(sw, lon_count)
    scale = weight(geometry(rows, 4)[2])
    band = 4 * rows

    def body(index, carry):
        at = pl.ds(pl.multiple_of(index * band, band), band)
        ahead, behind = lon_shifts(sw[at, :])
        main_ref[at, :] = ((ahead - behind) * scale)[:, :lon_count] + part_ref[at, :]
        return carry

    lax.fori_loop(0, RANK * rows // band, body, 0)


def halo_kernel(rows, main_ref, up_ref, down_ref, send_ref, keep_ref):
    wide = RANK * rows
    half = wide // 2
    me, beside = places()
    part, j = group(wide, rows, 0)
    per_piece = RANK // lax.axis_size("tm")
    piece, inner = group(wide, rows * per_piece, 0)[0], jnp.bitwise_and(part, per_piece - 1)
    if per_piece & (per_piece - 1):
        inner = part % per_piece
    mine = jnp.bitwise_xor(piece, me) * per_piece + inner
    theirs = real_column(iota((1, RANK), 1), beside)
    _, c_north, c_here, c_south = geometry(rows, RANK)
    hit = mine == theirs
    from_north = mm(one_hot(hit & (j == 0)), up_ref[...])
    from_south = mm(one_hot(hit & (j == rows - 1)), down_ref[...])
    total = main_ref[...] + weight(c_here) * (c_south * from_south - c_north * from_north)
    keep_ref[...] = total[:half]
    send_ref[...] = total[half:].astype(jnp.bfloat16)


def project_kernel(rows, lon_count, piece_count, *refs):
    piece_refs = refs[:piece_count]
    (up_ref, down_ref, east_ref, north_ref, sketch_ref, sums_ref, work, to_east, to_north) = refs[piece_count:]
    wide = RANK * rows
    piece_rows = piece_refs[0].shape[0]
    me, _ = places()
    start = 0
    for ref in piece_refs:
        for inner in range(ref.shape[0] // piece_rows):
            owner = jnp.bitwise_xor(me, start)
            at = pl.ds(pl.multiple_of(owner * piece_rows, piece_rows), piece_rows)
            sketch_ref[at, :] = ref[inner * piece_rows : (inner + 1) * piece_rows, :]
            start += 1
    work[:, :lon_count] = sketch_ref[...].astype(jnp.float32)
    wrap_columns(work, lon_count)
    band = 4 * rows
    j, c_north, c_here, c_south = geometry(rows, 4)
    scale = weight(c_here)
    above_scale = jnp.where(j == 0, 0.0, c_here * weight(c_north))
    below_scale = jnp.where(j == rows - 1, 0.0, -c_here * weight(c_south))

    def body(index, carry):
        at = pl.ds(pl.multiple_of(index * band, band), band)
        value = work[at, :]
        ahead, behind = lon_shifts(value)
        to_north[at, :] = ((behind - ahead) * scale)[:, :lon_count].astype(jnp.bfloat16)
        mixed = pltpu.roll(value, 1, 0) * above_scale + pltpu.roll(value, band - 1, 0) * below_scale
        to_east[at, :] = mixed[:, :lon_count].astype(jnp.bfloat16)
        return carry

    lax.fori_loop(0, wide // band, body, 0)
    fold = jnp.where(group(wide, rows, 1)[0] == iota((RANK, 1), 0), 1.0, 0.0)
    both = mm(east_ref[...], to_east[...], ((1,), (1,))) + mm(north_ref[...], to_north[...], ((1,), (1,)))
    slots = both.shape[0] // rows
    both = jnp.where(same_place(both.shape[0], wide, rows), both, 0.0)
    both = jnp.sum(both.reshape(slots, rows, wide), axis=1)
    terms = mm(fold, both, ((1,), (1,)), HIGHEST)
    value = sketch_ref[...]
    gram = jnp.where(same_place(wide, wide, rows), mm(value, value, ((1,), (1,))), 0.0)
    gram = mm(jnp.sum(gram.reshape(RANK, rows, wide), axis=1), fold, ((1,), (1,)), HIGHEST)
    _, c_north, c_here, c_south = geometry(1, 1)
    top = lax.axis_index("lat") * rows
    half = rows * lax.axis_size("lat") // 2

    def cosine(row):
        return jnp.cos(jnp.full((1, 1), half - row, jnp.int32).astype(jnp.float32) * (jnp.pi / 720.0))

    first = pick_rows(value, rows, 0) * (-cosine(top - 1) * weight(cosine(top)))
    last = pick_rows(value, rows, rows - 1) * (cosine(top + rows) * weight(cosine(top + rows - 1)))
    terms += mm(first.astype(jnp.bfloat16), up_ref[...], ((1,), (1,)))
    terms += mm(last.astype(jnp.bfloat16), down_ref[...], ((1,), (1,)))
    offset = sums_ref.shape[1] - 128
    sums_ref[...] = jnp.zeros_like(sums_ref)
    sums_ref[:, : terms.shape[1]] = terms
    sums_ref[:, offset : offset + RANK] = gram


def eliminate(table, block):
    down = iota((table.shape[0], 1), 0)
    for k in range(0, RANK, block):
        columns = [jnp.broadcast_to(table[:, k + i : k + i + 1], table.shape) for i in range(block)]
        lines = [table[k + i : k + i + 1, :] for i in range(block)]
        for i in range(block):
            inverse = 1.0 / columns[i][k + i : k + i + 1, :]
            for m in range(i + 1, block):
                ratio = columns[m][k + i : k + i + 1, :] * inverse
                lines[m] = lines[m] - ratio * lines[i]
                columns[m] = columns[m] - ratio * columns[i]
            table = table - jnp.where(down > k + i, columns[i] * inverse, 0.0) * lines[i]
    return table


def solve_kernel(rows, cell_total, count_ref, sums_ref, sketch_ref, basis_ref, coeffs_ref, work):
    scale = 1.0 / cell_total
    slots = coeffs_ref.shape[1]
    wide = RANK * rows
    offset = sums_ref.shape[1] - 128
    work[...] = jnp.where(iota(work.shape, 0) + RANK == iota(work.shape, 1), 1.0, 0.0)
    work[:, :RANK] = sums_ref[:, offset : offset + RANK] * scale
    table = eliminate(work[...], 4)
    diagonal = jnp.sum(jnp.where(iota((RANK, 1), 0) == iota((1, 128), 1), table, 0.0), axis=1, keepdims=True)
    work[...] = table * (1.0 / jnp.sqrt(diagonal))
    inverse = work[:, RANK : 2 * RANK]
    spread = spread_rows(rows)
    same = same_place(wide, wide, rows)
    high = inverse.astype(jnp.bfloat16)
    rest = inverse - high.astype(jnp.float32)
    middle = rest.astype(jnp.bfloat16)
    value = sketch_ref[...]

    def apply(part):
        tall = mm(spread, part).astype(jnp.bfloat16)
        large = jnp.where(same, mm(tall, spread, ((1,), (1,))), 0.0).astype(jnp.bfloat16)
        return mm(large, value)

    basis_ref[...] = (apply(high) + apply(middle)).astype(jnp.bfloat16)
    raw = mm(inverse, sums_ref[:, :slots], precision=HIGHEST) * scale
    coeffs_ref[...] = jnp.where(iota((1, slots), 1) < count_ref[0], raw, 0.0)


def partners(turn, bits, tm_count, lat_count):
    pairs = []
    for tm in range(tm_count):
        for lat in range(lat_count):
            bit = bit_order(lat, bits)[turn]
            pairs.append((tm * lat_count + lat, (tm ^ (1 << bit)) * lat_count + lat))
    return pairs


def local(wind_east, wind_north, snap_counts, snap_ids):
    slots, rows, lon_count = wind_east.shape
    tm_count, lat_count = lax.axis_size("tm"), lax.axis_size("lat")
    bits = tm_count.bit_length() - 1
    wide = RANK * rows
    cell_total = rows * lat_count * lon_count
    width = padded_width(lon_count)
    east = wind_east.reshape(slots * rows, lon_count)
    north = wind_north.reshape(slots * rows, lon_count)
    northward = [(i + 1, i) for i in range(lat_count - 1)]
    southward = [(i, i + 1) for i in range(lat_count - 1)]
    float_array = lambda *shape: jax.ShapeDtypeStruct(shape, jnp.float32)
    half_array = lambda *shape: jax.ShapeDtypeStruct(shape, jnp.bfloat16)

    part, up, down, signs = pl.pallas_call(
        functools.partial(east_kernel, rows, lon_count),
        in_specs=[SCALARS, FAR, FAR],
        out_specs=[WHOLE] * 4,
        out_shape=[
            float_array(wide, lon_count),
            half_array(RANK, lon_count),
            half_array(RANK, lon_count),
            half_array(wide, slots * rows),
        ],
        scratch_shapes=[
            pltpu.VMEM((1, slots), jnp.int32),
            pltpu.VMEM((slots * rows, lon_count), jnp.bfloat16),
            pltpu.VMEM((wide, width), jnp.float32),
            pltpu.SemaphoreType.DMA((3,)),
        ],
        compiler_params=params(),
        name="east_terms",
    )(snap_counts, in_hbm(snap_ids.reshape(1, slots)), in_hbm(east))
    above = lax.ppermute(up, "lat", southward)
    below = lax.ppermute(down, "lat", northward)
    main = pl.pallas_call(
        functools.partial(north_kernel, rows, lon_count),
        in_specs=[WHOLE] * 3,
        out_specs=WHOLE,
        out_shape=float_array(wide, lon_count),
        scratch_shapes=[pltpu.VMEM((wide, width), jnp.float32)],
        compiler_params=params(),
        name="north_terms",
    )(signs, part, north)
    send, keep = pl.pallas_call(
        functools.partial(halo_kernel, rows),
        in_specs=[WHOLE] * 3,
        out_specs=[WHOLE, WHOLE],
        out_shape=[half_array(wide // 2, lon_count), float_array(wide // 2, lon_count)],
        compiler_params=params(),
        name="halo_terms",
    )(main, above, below)

    edge_source, send = lax.optimization_barrier((wind_east, send))
    wind_above = lax.ppermute(edge_source[:, rows - 1, :], "lat", southward)
    wind_below = lax.ppermute(edge_source[:, 0, :], "lat", northward)

    both = ("tm", "lat")
    for turn in range(bits):
        got = lax.ppermute(send, both, partners(turn, bits, tm_count, lat_count))
        if turn == min(1, bits - 1):
            got, wind_above, wind_below = lax.optimization_barrier((got, wind_above, wind_below))
        keep = keep + got.astype(jnp.float32)
        if turn < bits - 1:
            half = keep.shape[0] // 2
            send, keep = keep[half:].astype(jnp.bfloat16), keep[:half]
    held = keep.astype(jnp.bfloat16)
    pieces = [held]
    for turn in reversed(range(bits)):
        got = lax.ppermute(held, both, partners(turn, bits, tm_count, lat_count))
        pieces.append(got)
        if turn:
            held = jnp.concatenate([held, got], axis=0)

    sums_width = -(-slots // 128) * 128 + 128
    sketch, sums = pl.pallas_call(
        functools.partial(project_kernel, rows, lon_count, len(pieces)),
        in_specs=[WHOLE] * (len(pieces) + 4),
        out_specs=[WHOLE, WHOLE],
        out_shape=[half_array(wide, lon_count), float_array(RANK, sums_width)],
        scratch_shapes=[
            pltpu.VMEM((wide, width), jnp.float32),
            pltpu.VMEM((wide, lon_count), jnp.bfloat16),
            pltpu.VMEM((wide, lon_count), jnp.bfloat16),
        ],
        compiler_params=params(),
        name="projection_terms",
    )(*pieces, wind_above, wind_below, east, north)

    shift = 1
    while shift < lat_count:
        sums = sums + lax.ppermute(sums, "lat", [(i, i ^ shift) for i in range(lat_count)])
        shift *= 2

    basis, coeffs = pl.pallas_call(
        functools.partial(solve_kernel, rows, cell_total),
        in_specs=[SCALARS, WHOLE, WHOLE],
        out_specs=[WHOLE, WHOLE],
        out_shape=[half_array(wide, lon_count), float_array(RANK, slots)],
        scratch_shapes=[pltpu.VMEM((RANK, 128), jnp.float32)],
        compiler_params=params(),
        name="basis_and_coeffs",
    )(snap_counts, sums, sketch)
    return basis.reshape(RANK, rows, lon_count), coeffs


def solution(mesh):
    in_specs = (P("tm", "lat", None), P("tm", "lat", None), P("tm"), P("tm"))
    out_specs = (P(None, "lat", None), P(None, "tm"))
    return jax.shard_map(local, mesh=mesh, in_specs=in_specs, out_specs=out_specs, check_vma=False)
```

time: 182 us -> 73.7 us (0.40)
  waiting for transfers between devices: 90.7 us -> 34.1 us
  local copies, waits for them, and re-layouts: 23.6 us -> 0.96 us
  blocking collectives: 22 us -> 0 us
  other arithmetic: 17 us -> 0.2 us
  starting transfers between devices: 4.44 us -> 21.1 us
  Pallas kernels: 0 us -> 15.5 us
  between operations: 15 us -> 1.59 us
  matrix products: 8.73 us -> 0 us
    psum x1 -> x0, waiting for transfers between devices: 90.7 us -> none  [local(): sketch = lax.psum(sketch, 'tm')]
    ppermute x2 -> x12, waiting for transfers between devices: 0.01 us -> 34.1 us  [the longest x3 18.7 us: local(): got = lax.ppermute(held, both, partners(turn, bits, tm_count, lat_count))]
    psum x2 -> x0, blocking collectives: 22 us -> none  [the longest x1 11.2 us: local(): gram_sum = lax.psum(local_gram(sketch, cell_total), 'lat')]
    ppermute x2 -> x12, starting transfers between devices: 4.4 us -> 21.1 us  [the longest x1 5.59 us: local(): wind_above = lax.ppermute(edge_source[:, rows - 1, :], 'lat', southward)]
    pallas_call x0 -> x5, Pallas kernels: none -> 15.5 us  [the longest x1 4.87 us: local(): pl.pallas_call(functools.partial(project_kernel, rows, lon_count, len(pie...]
    slice x3 -> x2, local copies, waits for them, and re-layouts: 10.9 us -> 0.04 us  [local(): send, keep = (keep[half:].astype(jnp.bfloat16), keep[:half])]
    dot_general x4 -> x0, matrix products: 8.51 us -> none  [the longest x1 3.17 us: local_gram(): lax.dot_general(sketch, sketch, (((1,), (1,)), ((), ())), precision=lax.P...]
    reshape x2 -> x0, local copies, waits for them, and re-layouts: 7.77 us -> none  [the longest x1 5.64 us: local(): metric_vorticity(padded_east, wind_north, padded_cosine, valid)]
  transfers between devices with their start and end apart: 3 -> 12, of which waited for: 1 -> 9; matrix products, arithmetic and copies ran while one was open for 5% -> 1% of each run, Pallas kernels for 0% -> 3%
where the time goes in v2:
time: 73.7 us; the launch traced here: 73.4 us
  waiting for transfers between devices  34.1 us (46%)
  starting transfers between devices  21.1 us (29%)
  Pallas kernels  15.5 us (21%)
  between operations  1.59 us (2%)
  local copies, waits for them, and re-layouts  0.96 us (1%)
    ppermute x3, waiting for transfers between devices, local(): got = lax.ppermute(held, both, partners(turn, bits, tm_count, lat_count))  18.7 us
    ppermute x3, waiting for transfers between devices, local(): got = lax.ppermute(send, both, partners(turn, bits, tm_count, lat_count))  10.2 us
    ppermute x1, starting transfers between devices, local(): wind_above = lax.ppermute(edge_source[:, rows - 1, :], 'lat', southward)  5.59 us
    pallas_call x1, Pallas kernels, local(): pl.pallas_call(functools.partial(project_kernel, rows, lon_count, len(pie...  4.87 us
    ppermute x3, starting transfers between devices, local(): got = lax.ppermute(send, both, partners(turn, bits, tm_count, lat_count))  4.73 us
    pallas_call x1, Pallas kernels, local(): pl.pallas_call(functools.partial(east_kernel, rows, lon_count), in_specs=...  3.47 us
    ppermute x2, starting transfers between devices, local(): lax.ppermute(sums, 'lat', [(i, i ^ shift) for i in range(lat_count)])  3.4 us
    ppermute x2, waiting for transfers between devices, local(): lax.ppermute(sums, 'lat', [(i, i ^ shift) for i in range(lat_count)])  3.13 us
  transfers between devices with their start and end apart: 12, of which 9 were waited for; matrix products, arithmetic and copies ran while one was open for 1% of the time, Pallas kernels for 3%

profile of v2, /device:TPU:0, one launch (start us, length us, event | category | flops | bytes accessed | tf_op | source)
XLA Modules:
  0.0 73.4 jit_solution(4357544509367802178)
XLA Ops:
  0.6 0.0 copy-start.1
  1.4 3.5 %east_terms.1 = (f32[256,1440]{1,0:T(8,128)S(1)}, bf16[32,1440]{1,0:T(8,128)(2,1)S(1)}, bf16[32,1440]{1,0:T(8,128)(2,1)S(1)}, bf16[256,960]{1,0:T(8,128)(2,1)S(1)}) custom-call(s32[1]{0:T(128)S(6)} %copy.8.count_ref, s32[1,120]{1,0:T(1,128)} %bitcast.12, bf16[960,1440]{1,0:T(8,128)(2,1)} %bitcast.8), custom_call_target="tpu_custom_call" | custom-call | tf_op jit(solution)/shard_map/east_terms/pallas_call | solution.py:323
  4.9 2.4 %collective-permute-start = (bf16[32,1440]{1,0:T(8,128)(2,1)S(1)}, bf16[32,1440]{1,0:T(8,128)(2,1)S(1)}, u32[]{:S(2)}, u32[]{:S(2)}) collective-permute-start(bf16[32,1440]{1,0:T(8,128)(2,1)S(1)} %get-tuple-element.19), channel_id=1, source_target_pairs={{0,1},{1,2},{2,3},{4,5},{5,6},{6,7},{8,9},{9,10},{10,11},{12,13},{... | collective-permute-start | bytes 276488 | tf_op jit(solution)/shard_map/ppermute | solution.py:342
  7.3 1.3 %collective-permute-start.1 = (bf16[32,1440]{1,0:T(8,128)(2,1)S(1)}, bf16[32,1440]{1,0:T(8,128)(2,1)S(1)}, u32[]{:S(2)}, u32[]{:S(2)}) collective-permute-start(bf16[32,1440]{1,0:T(8,128)(2,1)S(1)} %get-tuple-element.20), channel_id=1, source_target_pairs={{1,0},{2,1},{3,2},{5,4},{6,5},{7,6},{9,8},{10,9},{11,10},{13,12},{... | collective-permute-start | bytes 276488 | tf_op jit(solution)/shard_map/ppermute | solution.py:343
  8.6 0.0 copy-done.1
  8.6 0.0 copy-start
  8.6 2.5 %north_terms.1.main_ref = f32[256,1440]{1,0:T(8,128)S(1)} custom-call(bf16[256,960]{1,0:T(8,128)(2,1)S(1)} %get-tuple-element.17.signs_ref, f32[256,1440]{1,0:T(8,128)S(1)} %get-tuple-element.18.part_ref, bf16[960,1440]{1,0:T(8,128)(2,1)S(1)} %bitcast.10), custom_call_target="tpu_custom_call" | custom-call | tf_op jit(solution)/shard_map/north_terms/pallas_call | solution.py:344
  11.1 0.0 collective-permute-done.up_ref
  11.1 1.5 %collective-permute-done.1.down_ref = bf16[32,1440]{1,0:T(8,128)(2,1)S(1)} collective-permute-done((bf16[32,1440]{1,0:T(8,128)(2,1)S(1)}, bf16[32,1440]{1,0:T(8,128)(2,1)S(1)}, u32[]{:S(2)}, u32[]{:S(2)}) %collective-permute-start.1) | collective-permute-done | bytes 92192 | tf_op jit(solution)/shard_map/ppermute | solution.py:343
  12.6 1.9 %halo_terms.1 = (bf16[128,1440]{1,0:T(8,128)(2,1)S(1)}, f32[128,1440]{1,0:T(8,128)S(1)}) custom-call(f32[256,1440]{1,0:T(8,128)S(1)} %north_terms.1.main_ref, bf16[32,1440]{1,0:T(8,128)(2,1)S(1)} %collective-permute-done.up_ref, bf16[32,1440]{1,0:T(8,128)(2,1)S(1)} %collective-permute-done.1.down_ref), custom_call_target="tpu_custom_call" | custom-call | tf_op jit(solution)/shard_map/halo_terms/pallas_call | solution.py:353
  14.5 1.6 %collective-permute-start.2 = (bf16[128,1440]{1,0:T(8,128)(2,1)S(1)}, bf16[128,1440]{1,0:T(8,128)(2,1)S(1)}, u32[]{:S(2)}, u32[]{:S(2)}) collective-permute-start(bf16[128,1440]{1,0:T(8,128)(2,1)S(1)} %get-tuple-element.23), channel_id=1, source_target_pairs={{0,4},{1,9},{2,6},{3,11},{4,0},{5,13},{6,2},{7,15},{8,12},{9,1},{1... | collective-permute-start | bytes 1105928 | tf_op jit(solution)/shard_map/ppermute | solution.py:368
  16.1 0.0 copy-done
  16.1 0.9 %copy.6 = bf16[120,8,1440]{2,0,1:T(8,128)(2,1)S(1)} copy(bf16[120,8,1440]{2,1,0:T(8,128)(2,1)S(1)} %copy-done) | data formatting | bytes 5529600 | tf_op jit(solution)/shard_map/optimization_barrier | solution.py:362
  16.9 0.1 slice_bitcast_fusion
  17.0 1.3 %collective-permute-start.5 = (bf16[120,1440]{1,0:T(8,128)(2,1)S(1)}, bf16[120,1440]{1,0:T(8,128)(2,1)S(1)}, u32[]{:S(2)}, u32[]{:S(2)}) collective-permute-start(bf16[120,1440]{1,0:T(8,128)(2,1)S(1)} %get-tuple-element.32), channel_id=1, source_target_pairs={{1,0},{2,1},{3,2},{5,4},{6,5},{7,6},{9,8},{10,9},{11,10},{13,12},{... | collective-permute-start | bytes 1036808 | tf_op jit(solution)/shard_map/ppermute | solution.py:364
  18.3 5.6 %collective-permute-start.4 = (bf16[120,1440]{1,0:T(8,128)(2,1)S(1)}, bf16[120,1440]{1,0:T(8,128)(2,1)S(1)}, u32[]{:S(2)}, u32[]{:S(2)}) collective-permute-start(bf16[120,1440]{1,0:T(8,128)(2,1)S(1)} %get-tuple-element.33), channel_id=1, source_target_pairs={{0,1},{1,2},{2,3},{4,5},{5,6},{6,7},{8,9},{9,10},{10,11},{12,13},{... | collective-permute-start | bytes 1036808 | tf_op jit(solution)/shard_map/ppermute | solution.py:363
  23.9 0.0 collective-permute-done.2
  23.9 0.1 convert_add_fusion
  24.0 0.5 collective-permute-start.3
  24.6 0.0 collective-permute-done.5.refs_5_
  24.6 0.6 collective-permute-done.4.refs_4_
  25.2 4.6 %collective-permute-done.3 = bf16[64,1440]{1,0:T(8,128)(2,1)S(1)} collective-permute-done((bf16[64,1440]{1,0:T(8,128)(2,1)S(1)}, bf16[64,1440]{1,0:T(8,128)(2,1)S(1)}, u32[]{:S(2)}, u32[]{:S(2)}) %collective-permute-start.3) | collective-permute-done | bytes 184352 | tf_op jit(solution)/shard_map/ppermute | solution.py:368
  29.8 2.7 %collective-permute-start.6 = (bf16[32,1440]{1,0:T(8,128)(2,1)S(1)}, bf16[32,1440]{1,0:T(8,128)(2,1)S(1)}, u32[]{:S(2)}, u32[]{:S(2)}) collective-permute-start(bf16[32,1440]{1,0:T(8,128)(2,1)S(1)} %slice.41), channel_id=1, source_target_pairs={{0,16},{1,17},{2,18},{3,19},{4,20},{5,21},{6,22},{7,23},{8,24},{9,... | collective-permute-start | bytes 276488 | tf_op jit(solution)/shard_map/ppermute | solution.py:368
  32.5 5.6 %collective-permute-done.6 = bf16[32,1440]{1,0:T(8,128)(2,1)S(1)} collective-permute-done((bf16[32,1440]{1,0:T(8,128)(2,1)S(1)}, bf16[32,1440]{1,0:T(8,128)(2,1)S(1)}, u32[]{:S(2)}, u32[]{:S(2)}) %collective-permute-start.6) | collective-permute-done | bytes 92192 | tf_op jit(solution)/shard_map/ppermute | solution.py:368
  38.1 0.8 %collective-permute-start.7 = (bf16[32,1440]{1,0:T(8,128)(2,1)S(1)}, bf16[32,1440]{1,0:T(8,128)(2,1)S(1)}, u32[]{:S(2)}, u32[]{:S(2)}) collective-permute-start(bf16[32,1440]{1,0:T(8,128)(2,1)S(1)} %fusion.refs_0_), channel_id=1, source_target_pairs={{0,16},{1,17},{2,18},{3,19},{4,20},{5,21},{6,22},{7,23},{8,24},{9,... | collective-permute-start | bytes 276488 | tf_op jit(solution)/shard_map/ppermute | solution.py:378
  38.8 6.8 %collective-permute-done.7.refs_1_ = bf16[32,1440]{1,0:T(8,128)(2,1)S(1)} collective-permute-done((bf16[32,1440]{1,0:T(8,128)(2,1)S(1)}, bf16[32,1440]{1,0:T(8,128)(2,1)S(1)}, u32[]{:S(2)}, u32[]{:S(2)}) %collective-permute-start.7) | collective-permute-done | bytes 92192 | tf_op jit(solution)/shard_map/ppermute | solution.py:378
  45.6 0.1 collective-permute-start.8
  45.7 5.7 %collective-permute-done.8.refs_2_ = bf16[64,1440]{1,0:T(8,128)(2,1)S(1)} collective-permute-done((bf16[64,1440]{1,0:T(8,128)(2,1)S(1)}, bf16[64,1440]{1,0:T(8,128)(2,1)S(1)}, u32[]{:S(2)}, u32[]{:S(2)}) %collective-permute-start.8) | collective-permute-done | bytes 184352 | tf_op jit(solution)/shard_map/ppermute | solution.py:378
  51.4 1.6 %collective-permute-start.9 = (bf16[128,1440]{1,0:T(8,128)(2,1)S(1)}, bf16[128,1440]{1,0:T(8,128)(2,1)S(1)}, u32[]{:S(2)}, u32[]{:S(2)}) collective-permute-start(bf16[128,1440]{1,0:T(8,128)(2,1)S(1)} %pad_maximum_fusion), channel_id=1, source_target_pairs={{0,4},{1,9},{2,6},{3,11},{4,0},{5,13},{6,2},{7,15},{8,12},{9,1},{1... | collective-permute-start | bytes 1105928 | tf_op jit(solution)/shard_map/ppermute | solution.py:378
  52.9 6.3 %collective-permute-done.9.refs_3_ = bf16[128,1440]{1,0:T(8,128)(2,1)S(1)} collective-permute-done((bf16[128,1440]{1,0:T(8,128)(2,1)S(1)}, bf16[128,1440]{1,0:T(8,128)(2,1)S(1)}, u32[]{:S(2)}, u32[]{:S(2)}) %collective-permute-start.9) | collective-permute-done | bytes 368672 | tf_op jit(solution)/shard_map/ppermute | solution.py:378
  59.2 4.9 %projection_terms.1 = (bf16[256,1440]{1,0:T(8,128)(2,1)S(1)}, f32[32,256]{1,0:T(8,128)S(1)}) custom-call(bf16[32,1440]{1,0:T(8,128)(2,1)S(1)} %fusion.refs_0_, bf16[32,1440]{1,0:T(8,128)(2,1)S(1)} %collective-permute-done.7.refs_1_, bf16[64,1440]{1,0:T(8,128)(2,1)S(1)} %collective-permute-done.8.refs_2_, ...), custom_call_target="tpu_custom_call" | custom-call | tf_op jit(solution)/shard_map/projection_terms/pallas_call | solution.py:384
  64.1 0.0 collective-permute-start.10
  64.1 1.2 %collective-permute-done.10 = f32[32,256]{1,0:T(8,128)S(1)} collective-permute-done((f32[32,256]{1,0:T(8,128)S(1)}, f32[32,256]{1,0:T(8,128)S(1)}, u32[]{:S(2)}, u32[]{:S(2)}) %collective-permute-start.10) | collective-permute-done | bytes 32800 | tf_op jit(solution)/shard_map/ppermute | solution.py:400
  65.3 3.4 %collective-permute-start.11 = (f32[32,256]{1,0:T(8,128)S(1)}, f32[32,256]{1,0:T(8,128)S(1)}, u32[]{:S(2)}, u32[]{:S(2)}) collective-permute-start(f32[32,256]{1,0:T(8,128)S(1)} %add.18), channel_id=1, source_target_pairs={{0,2},{1,3},{2,0},{3,1},{4,6},{5,7},{6,4},{7,5},{8,10},{9,11},{10,... | collective-permute-start | bytes 98312 | tf_op jit(solution)/shard_map/ppermute | solution.py:400
  68.7 1.9 %collective-permute-done.11 = f32[32,256]{1,0:T(8,128)S(1)} collective-permute-done((f32[32,256]{1,0:T(8,128)S(1)}, f32[32,256]{1,0:T(8,128)S(1)}, u32[]{:S(2)}, u32[]{:S(2)}) %collective-permute-start.11) | collective-permute-done | bytes 32800 | tf_op jit(solution)/shard_map/ppermute | solution.py:400
  70.6 2.8 %basis_and_coeffs.1 = (bf16[256,1440]{1,0:T(8,128)(2,1)}, f32[32,120]{1,0:T(8,128)}) custom-call(s32[1]{0:T(128)S(6)} %copy.8.count_ref, f32[32,256]{1,0:T(8,128)S(1)} %add.19.sums_ref, bf16[256,1440]{1,0:T(8,128)(2,1)S(1)} %get-tuple-element.29.sketch_ref), custom_call_target="tpu_custom_call" | custom-call | tf_op jit(solution)/shard_map/basis_and_coeffs/pallas_call | solution.py:403
  (8 shorter events, 0.2 us)
Async XLA Ops:
  0.6 8.0 %copy-start.1 = (bf16[120,8,1440]{2,1,0:T(8,128)(2,1)S(1)}, bf16[120,8,1440]{2,1,0:T(8,128)(2,1)}, u32[]{:S(2)}) copy-start(bf16[120,8,1440]{2,1,0:T(8,128)(2,1)} %param.5) | copy-start | bytes 8294404
  4.9 6.2 %collective-permute-start = (bf16[32,1440]{1,0:T(8,128)(2,1)S(1)}, bf16[32,1440]{1,0:T(8,128)(2,1)S(1)}, u32[]{:S(2)}, u32[]{:S(2)}) collective-permute-start(bf16[32,1440]{1,0:T(8,128)(2,1)S(1)} %get-tuple-element.19), channel_id=1, source_target_pairs={{0,1},{1,2},{2,3},{4,5},{5,6},{6,7},{8,9},{9,10},{10,11},{12,13},{... | collective-permute-start | bytes 276488 | tf_op jit(solution)/shard_map/ppermute | solution.py:342
  7.3 5.3 %collective-permute-start.1 = (bf16[32,1440]{1,0:T(8,128)(2,1)S(1)}, bf16[32,1440]{1,0:T(8,128)(2,1)S(1)}, u32[]{:S(2)}, u32[]{:S(2)}) collective-permute-start(bf16[32,1440]{1,0:T(8,128)(2,1)S(1)} %get-tuple-element.20), channel_id=1, source_target_pairs={{1,0},{2,1},{3,2},{5,4},{6,5},{7,6},{9,8},{10,9},{11,10},{13,12},{... | collective-permute-start | bytes 276488 | tf_op jit(solution)/shard_map/ppermute | solution.py:343
  8.6 7.5 %copy-start = (bf16[120,8,1440]{2,1,0:T(8,128)(2,1)S(1)}, bf16[120,8,1440]{2,1,0:T(8,128)(2,1)}, u32[]{:S(2)}) copy-start(bf16[120,8,1440]{2,1,0:T(8,128)(2,1)} %param.4) | copy-start | bytes 8294404
  14.5 9.4 %collective-permute-start.2 = (bf16[128,1440]{1,0:T(8,128)(2,1)S(1)}, bf16[128,1440]{1,0:T(8,128)(2,1)S(1)}, u32[]{:S(2)}, u32[]{:S(2)}) collective-permute-start(bf16[128,1440]{1,0:T(8,128)(2,1)S(1)} %get-tuple-element.23), channel_id=1, source_target_pairs={{0,4},{1,9},{2,6},{3,11},{4,0},{5,13},{6,2},{7,15},{8,12},{9,1},{1... | collective-permute-start | bytes 1105928 | tf_op jit(solution)/shard_map/ppermute | solution.py:368
  17.0 7.6 %collective-permute-start.5 = (bf16[120,1440]{1,0:T(8,128)(2,1)S(1)}, bf16[120,1440]{1,0:T(8,128)(2,1)S(1)}, u32[]{:S(2)}, u32[]{:S(2)}) collective-permute-start(bf16[120,1440]{1,0:T(8,128)(2,1)S(1)} %get-tuple-element.32), channel_id=1, source_target_pairs={{1,0},{2,1},{3,2},{5,4},{6,5},{7,6},{9,8},{10,9},{11,10},{13,12},{... | collective-permute-start | bytes 1036808 | tf_op jit(solution)/shard_map/ppermute | solution.py:364
  18.3 6.9 %collective-permute-start.4 = (bf16[120,1440]{1,0:T(8,128)(2,1)S(1)}, bf16[120,1440]{1,0:T(8,128)(2,1)S(1)}, u32[]{:S(2)}, u32[]{:S(2)}) collective-permute-start(bf16[120,1440]{1,0:T(8,128)(2,1)S(1)} %get-tuple-element.33), channel_id=1, source_target_pairs={{0,1},{1,2},{2,3},{4,5},{5,6},{6,7},{8,9},{9,10},{10,11},{12,13},{... | collective-permute-start | bytes 1036808 | tf_op jit(solution)/shard_map/ppermute | solution.py:363
  24.0 5.7 %collective-permute-start.3 = (bf16[64,1440]{1,0:T(8,128)(2,1)S(1)}, bf16[64,1440]{1,0:T(8,128)(2,1)S(1)}, u32[]{:S(2)}, u32[]{:S(2)}) collective-permute-start(bf16[64,1440]{1,0:T(8,128)(2,1)S(1)} %slice.40), channel_id=1, source_target_pairs={{0,8},{1,5},{2,10},{3,7},{4,12},{5,1},{6,14},{7,3},{8,0},{9,13},{1... | collective-permute-start | bytes 552968 | tf_op jit(solution)/shard_map/ppermute | solution.py:368
  29.8 8.2 %collective-permute-start.6 = (bf16[32,1440]{1,0:T(8,128)(2,1)S(1)}, bf16[32,1440]{1,0:T(8,128)(2,1)S(1)}, u32[]{:S(2)}, u32[]{:S(2)}) collective-permute-start(bf16[32,1440]{1,0:T(8,128)(2,1)S(1)} %slice.41), channel_id=1, source_target_pairs={{0,16},{1,17},{2,18},{3,19},{4,20},{5,21},{6,22},{7,23},{8,24},{9,... | collective-permute-start | bytes 276488 | tf_op jit(solution)/shard_map/ppermute | solution.py:368
  38.1 7.5 %collective-permute-start.7 = (bf16[32,1440]{1,0:T(8,128)(2,1)S(1)}, bf16[32,1440]{1,0:T(8,128)(2,1)S(1)}, u32[]{:S(2)}, u32[]{:S(2)}) collective-permute-start(bf16[32,1440]{1,0:T(8,128)(2,1)S(1)} %fusion.refs_0_), channel_id=1, source_target_pairs={{0,16},{1,17},{2,18},{3,19},{4,20},{5,21},{6,22},{7,23},{8,24},{9,... | collective-permute-start | bytes 276488 | tf_op jit(solution)/shard_map/ppermute | solution.py:378
  45.6 5.7 %collective-permute-start.8 = (bf16[64,1440]{1,0:T(8,128)(2,1)S(1)}, bf16[64,1440]{1,0:T(8,128)(2,1)S(1)}, u32[]{:S(2)}, u32[]{:S(2)}) collective-permute-start(bf16[64,1440]{1,0:T(8,128)(2,1)S(1)} %pad_maximum_fusion.1), channel_id=1, source_target_pairs={{0,8},{1,5},{2,10},{3,7},{4,12},{5,1},{6,14},{7,3},{8,0},{9,13},{1... | collective-permute-start | bytes 552968 | tf_op jit(solution)/shard_map/ppermute | solution.py:378
  51.4 7.8 %collective-permute-start.9 = (bf16[128,1440]{1,0:T(8,128)(2,1)S(1)}, bf16[128,1440]{1,0:T(8,128)(2,1)S(1)}, u32[]{:S(2)}, u32[]{:S(2)}) collective-permute-start(bf16[128,1440]{1,0:T(8,128)(2,1)S(1)} %pad_maximum_fusion), channel_id=1, source_target_pairs={{0,4},{1,9},{2,6},{3,11},{4,0},{5,13},{6,2},{7,15},{8,12},{9,1},{1... | collective-permute-start | bytes 1105928 | tf_op jit(solution)/shard_map/ppermute | solution.py:378
  64.1 1.2 %collective-permute-start.10 = (f32[32,256]{1,0:T(8,128)S(1)}, f32[32,256]{1,0:T(8,128)S(1)}, u32[]{:S(2)}, u32[]{:S(2)}) collective-permute-start(f32[32,256]{1,0:T(8,128)S(1)} %get-tuple-element.28), channel_id=1, source_target_pairs={{0,1},{1,0},{2,3},{3,2},{4,5},{5,4},{6,7},{7,6},{8,9},{9,8},{10,11... | collective-permute-start | bytes 98312 | tf_op jit(solution)/shard_map/ppermute | solution.py:400
  65.3 5.3 %collective-permute-start.11 = (f32[32,256]{1,0:T(8,128)S(1)}, f32[32,256]{1,0:T(8,128)S(1)}, u32[]{:S(2)}, u32[]{:S(2)}) collective-permute-start(f32[32,256]{1,0:T(8,128)S(1)} %add.18), channel_id=1, source_target_pairs={{0,2},{1,3},{2,0},{3,1},{4,6},{5,7},{6,4},{7,5},{8,10},{9,11},{10,... | collective-permute-start | bytes 98312 | tf_op jit(solution)/shard_map/ppermute | solution.py:400

commit v3 on v2

v3 whole, which is shorter than its diff:
```python
import functools

import jax
import jax.numpy as jnp
from jax import lax
from jax.experimental import pallas as pl
from jax.experimental.pallas import tpu as pltpu
from jax.sharding import PartitionSpec as P

RANK = 32
VMEM_LIMIT = 32 * 1024 * 1024
HIGHEST = lax.Precision.HIGHEST
WHOLE = pl.BlockSpec(memory_space=pltpu.VMEM)
SCALARS = pl.BlockSpec(memory_space=pltpu.SMEM)
FAR = pl.BlockSpec(memory_space=pltpu.HBM)


def in_hbm(array):
    return pltpu.with_memory_space_constraint(array, pltpu.HBM)


def params():
    return pltpu.CompilerParams(vmem_limit_bytes=VMEM_LIMIT)


def mm(a, b, dims=((1,), (0,)), precision=None):
    return lax.dot_general(a, b, (dims, ((), ())), precision=precision, preferred_element_type=jnp.float32)


def iota(shape, axis):
    return lax.broadcasted_iota(jnp.int32, shape, axis)


def one_hot(condition):
    return jnp.where(condition, 1.0, 0.0).astype(jnp.bfloat16)


def group(count, rows, axis):
    index = iota((count, 1) if axis == 0 else (1, count), axis)
    if rows & (rows - 1) == 0:
        return jnp.right_shift(index, rows.bit_length() - 1), jnp.bitwise_and(index, rows - 1)
    return index // rows, index % rows


def spread_rows(rows):
    return one_hot(group(RANK * rows, rows, 0)[0] == iota((1, RANK), 1))


def same_place(tall, wide, rows):
    return group(tall, rows, 0)[1] == group(wide, rows, 1)[1]


def pick_rows(value, rows, j):
    tall = value.shape[0]
    return mm(one_hot(iota((1, tall), 1) == iota((tall // rows, 1), 0) * rows + j), value)


def padded_width(lon_count):
    return lon_count if lon_count % 128 == 0 else (lon_count + 2 + 127) // 128 * 128


def lon_shifts(value):
    return pltpu.roll(value, value.shape[1] - 1, 1), pltpu.roll(value, 1, 1)


def wrap_columns(ref, lon_count):
    width = ref.shape[1]
    if width != lon_count:
        ref[:, lon_count : lon_count + 1] = ref[:, 0:1]
        ref[:, width - 1 : width] = ref[:, lon_count - 1 : lon_count]


def bit_order(lat, bits):
    order = list(range(bits))
    if lat % 2 and bits > 1:
        order[0], order[1] = order[1], order[0]
    return order


def relative_place(tm, parity, bits):
    def place(order):
        total = 0
        for turn, bit in enumerate(order):
            total = total + (((tm >> bit) & 1) << (bits - 1 - turn))
        return total
    return jnp.where(parity == 1, place(bit_order(1, bits)), place(bit_order(0, bits)))


def places():
    bits = lax.axis_size("tm").bit_length() - 1
    tm, parity = lax.axis_index("tm"), jnp.bitwise_and(lax.axis_index("lat"), 1)
    return relative_place(tm, parity, bits), relative_place(tm, 1 - parity, bits)


def real_column(order, place):
    per_piece = RANK // lax.axis_size("tm")
    part, inner = group(RANK, per_piece, 0 if order.shape[1] == 1 else 1)
    if order.shape[0] * order.shape[1] != RANK:
        part, inner = order // per_piece, order % per_piece
    return jnp.bitwise_xor(part, place) * per_piece + inner


def cosine(row, total_rows):
    return jnp.cos((total_rows // 2 - row).astype(jnp.float32) * (jnp.pi / 720.0))


def weight(cosines):
    return 0.5 / jnp.sqrt(cosines)


def geometry(rows, repeat):
    total_rows = rows * lax.axis_size("lat")
    j = iota((rows, 1), 0)
    here = lax.axis_index("lat") * rows + j
    columns = [j] + [cosine(here + step, total_rows) for step in (-1, 0, 1)]
    return [jnp.concatenate([column] * repeat, axis=0) for column in columns]


def lat_shifts(value, rows):
    grouped = value.reshape(value.shape[0] // rows, rows, value.shape[1])
    return [pltpu.roll(grouped, by, 1).reshape(value.shape) for by in (1, rows - 1)]


def sketch_kernel(
    rows, lon_count, count_ref, ids_hbm, east_hbm, north_hbm, send_ref, keep_ref, up_near, up_far, down_near, down_far,
    signs_ref, ids, east, north, se, sw, sems
):
    slots = ids.shape[1]
    wide = RANK * rows
    cut = slots * rows // 32 * 16
    pieces = [pl.ds(0, cut), pl.ds(cut, slots * rows - cut)]
    keys = pltpu.make_async_copy(ids_hbm, ids, sems.at[4])
    keys.start()
    copies = []
    for source, target in ((east_hbm, east), (north_hbm, north)):
        for at in pieces:
            copy = pltpu.make_async_copy(source.at[at], target.at[at], sems.at[len(copies)])
            copy.start()
            copies.append(copy)
    me, beside = places()
    column = real_column(iota((RANK, 1), 0), me)
    spread = spread_rows(rows)
    across = one_hot(group(slots * rows, rows, 1)[0] == iota((slots, 1), 0))
    j, c_north, c_here, c_south = geometry(rows, 4)
    scale = weight(c_here)
    above_scale = jnp.where(j == 0, 0.0, -c_north * scale)
    below_scale = jnp.where(j == rows - 1, 0.0, c_south * scale)
    keys.wait()
    mixed = ids[...] * 1103515245 + (column * 40503 + 12345)
    mixed = jnp.bitwise_xor(mixed, jnp.right_shift(mixed, 13))
    mixed = mixed * 1664525 + 1013904223
    mixed = jnp.bitwise_xor(mixed, jnp.right_shift(mixed, 16))
    flipped = jnp.bitwise_and(jnp.right_shift(mixed, 7), 1)
    used = iota((1, slots), 1) < count_ref[0]
    signs = jnp.where(used, 1 - 2 * flipped, 0).astype(jnp.float32).astype(jnp.bfloat16)
    full = mm(mm(spread, signs).astype(jnp.bfloat16), across)
    signs_ref[...] = jnp.where(same_place(wide, slots * rows, rows), full, 0.0).astype(jnp.bfloat16)
    copies[0].wait()
    se[:, :lon_count] = mm(signs_ref[:, :cut], east[:cut, :])
    copies[1].wait()
    se[:, :lon_count] += mm(signs_ref[:, cut:], east[cut:, :])
    rounded = se[:, :lon_count].astype(jnp.bfloat16)
    order = real_column(iota((RANK, 1), 0), beside)
    tall_part, tall_place = group(wide, rows, 1)
    per_piece = RANK // lax.axis_size("tm")
    own = group(wide, rows * per_piece, 1)[0]
    own = jnp.bitwise_xor(own, me) * per_piece + (tall_part - own * per_piece)
    for row, near, far in ((rows - 1, up_near, up_far), (0, down_near, down_far)):
        edge = mm(one_hot((order == own) & (tall_place == row)), rounded).astype(jnp.bfloat16)
        near[...] = edge[: RANK // 2]
        far[...] = edge[RANK // 2 :]
    copies[2].wait()
    sw[:, :lon_count] = mm(signs_ref[:, :cut], north[:cut, :])
    copies[3].wait()
    sw[:, :lon_count] += mm(signs_ref[:, cut:], north[cut:, :])
    wrap_columns(sw, lon_count)
    band = 4 * rows
    for index in range(wide // band):
        at = slice(index * band, (index + 1) * band)
        ahead, behind = lon_shifts(sw[at, :])
        above, below = lat_shifts(se[at, :lon_count], rows)
        total = ((ahead - behind) * scale)[:, :lon_count] + above * above_scale + below * below_scale
        if index * band < wide // 2:
            keep_ref[at, :] = total
        else:
            send_ref[index * band - wide // 2 : (index + 1) * band - wide // 2, :] = total.astype(jnp.bfloat16)


def halo_kernel(rows, keep_ref, got_ref, up_near, up_far, down_near, down_far, send_ref, held_ref):
    tall = keep_ref.shape[0]
    edge_rows = tall // rows
    part, j = group(tall, rows, 0)
    source, column = group(4 * edge_rows, edge_rows, 1)
    goes = jnp.where(source < 2, 0, rows - 1)
    place = one_hot((part == column) & (j == goes))
    j, c_north, c_here, c_south = geometry(rows, 1)
    scale = weight(c_here) * jnp.where(j == 0, -c_north, c_south)
    scale = jnp.concatenate([scale] * edge_rows, axis=0)
    edges = jnp.concatenate([up_near[...], up_far[...], down_near[...], down_far[...]], axis=0)
    total = keep_ref[...] + got_ref[...].astype(jnp.float32) + scale * mm(place, edges)
    held_ref[...] = total[: tall // 2]
    send_ref[...] = total[tall // 2 :].astype(jnp.bfloat16)


def stencil_adjoint(rows, lon_count, work, to_east, to_north):
    band = 4 * rows
    j, c_north, c_here, c_south = geometry(rows, 4)
    scale = weight(c_here)
    above_scale = jnp.where(j == 0, 0.0, c_here * weight(c_north))
    below_scale = jnp.where(j == rows - 1, 0.0, -c_here * weight(c_south))
    for index in range(work.shape[0] // band):
        at = slice(index * band, (index + 1) * band)
        value = work[at, :]
        ahead, behind = lon_shifts(value)
        to_north[at, :] = ((behind - ahead) * scale)[:, :lon_count].astype(jnp.bfloat16)
        above, below = lat_shifts(value, rows)
        to_east[at, :] = (above * above_scale + below * below_scale)[:, :lon_count].astype(jnp.bfloat16)


def project_kernel(rows, lon_count, piece_ref, up_ref, down_ref, east_ref, north_ref, terms_ref, work, to_east, to_north):
    tall = piece_ref.shape[0]
    columns = tall // rows
    value = piece_ref[...]
    work[:, :lon_count] = value.astype(jnp.float32)
    wrap_columns(work, lon_count)
    stencil_adjoint(rows, lon_count, work, to_east, to_north)
    both = mm(east_ref[...], to_east[...], ((1,), (1,))) + mm(north_ref[...], to_north[...], ((1,), (1,)))
    slots = both.shape[0] // rows
    both = jnp.where(same_place(both.shape[0], tall, rows), both, 0.0)
    both = jnp.sum(both.reshape(slots, rows, tall), axis=1)
    fold = jnp.where(group(tall, rows, 1)[0] == iota((columns, 1), 0), 1.0, 0.0)
    terms = mm(fold, both, ((1,), (1,)), HIGHEST)
    total_rows = rows * lax.axis_size("lat")
    top = jnp.full((1, 1), lax.axis_index("lat") * rows, jnp.int32)
    first_scale = -cosine(top - 1, total_rows) * weight(cosine(top, total_rows))
    last_scale = cosine(top + rows, total_rows) * weight(cosine(top + rows - 1, total_rows))
    first = pick_rows(value, rows, 0) * first_scale
    last = pick_rows(value, rows, rows - 1) * last_scale
    terms += mm(first.astype(jnp.bfloat16), up_ref[...], ((1,), (1,)))
    terms += mm(last.astype(jnp.bfloat16), down_ref[...], ((1,), (1,)))
    terms_ref[...] = jnp.zeros_like(terms_ref)
    terms_ref[:, : terms.shape[1]] = terms


def gather_kernel(rows, piece_rows, first_ref, second_ref, head_ref, tail_ref, sketch_ref, sums_ref):
    wide = RANK * rows
    me, _ = places()
    start = 0
    for ref in (first_ref, second_ref):
        for inner in range(ref.shape[0] // piece_rows):
            owner = jnp.bitwise_xor(me, start)
            at = pl.ds(pl.multiple_of(owner * piece_rows, piece_rows), piece_rows)
            sketch_ref[at, :] = ref[inner * piece_rows : (inner + 1) * piece_rows, :]
            start += 1
    value = sketch_ref[...]
    fold = jnp.where(group(wide, rows, 1)[0] == iota((RANK, 1), 0), 1.0, 0.0)
    gram = jnp.where(same_place(wide, wide, rows), mm(value, value, ((1,), (1,))), 0.0)
    gram = mm(jnp.sum(gram.reshape(RANK, rows, wide), axis=1), fold, ((1,), (1,)), HIGHEST)
    turn = jnp.where(iota((RANK, 1), 0) == real_column(iota((1, RANK), 1), me), 1.0, 0.0)
    half = RANK // 2
    terms = mm(turn, jnp.concatenate([head_ref[...], tail_ref[...]], axis=0), precision=HIGHEST)
    offset = sums_ref.shape[1] - 128
    sums_ref[:, :offset] = terms
    sums_ref[:, offset:] = jnp.zeros((RANK, 128), jnp.float32)
    sums_ref[:, offset : offset + RANK] = gram


def eliminate(table, block):
    down = iota((table.shape[0], 1), 0)
    for k in range(0, RANK, block):
        columns = [jnp.broadcast_to(table[:, k + i : k + i + 1], table.shape) for i in range(block)]
        lines = [table[k + i : k + i + 1, :] for i in range(block)]
        for i in range(block):
            inverse = 1.0 / columns[i][k + i : k + i + 1, :]
            for m in range(i + 1, block):
                ratio = columns[m][k + i : k + i + 1, :] * inverse
                lines[m] = lines[m] - ratio * lines[i]
                columns[m] = columns[m] - ratio * columns[i]
            table = table - jnp.where(down > k + i, columns[i] * inverse, 0.0) * lines[i]
    return table


def solve_kernel(rows, cell_total, count_ref, sums_ref, sketch_ref, basis_ref, coeffs_ref, work):
    scale = 1.0 / cell_total
    slots = coeffs_ref.shape[1]
    wide = RANK * rows
    offset = sums_ref.shape[1] - 128
    work[...] = jnp.where(iota(work.shape, 0) + RANK == iota(work.shape, 1), 1.0, 0.0)
    work[:, :RANK] = sums_ref[:, offset : offset + RANK] * scale
    table = eliminate(work[...], 4)
    diagonal = jnp.sum(jnp.where(iota((RANK, 1), 0) == iota((1, 128), 1), table, 0.0), axis=1, keepdims=True)
    work[...] = table * (1.0 / jnp.sqrt(diagonal))
    inverse = work[:, RANK : 2 * RANK]
    spread = spread_rows(rows)
    same = same_place(wide, wide, rows)
    high = inverse.astype(jnp.bfloat16)
    rest = inverse - high.astype(jnp.float32)
    middle = rest.astype(jnp.bfloat16)
    value = sketch_ref[...]

    def apply(part):
        tall = mm(spread, part).astype(jnp.bfloat16)
        large = jnp.where(same, mm(tall, spread, ((1,), (1,))), 0.0).astype(jnp.bfloat16)
        return mm(large, value)

    basis_ref[...] = (apply(high) + apply(middle)).astype(jnp.bfloat16)
    raw = mm(inverse, sums_ref[:, :slots], precision=HIGHEST) * scale
    coeffs_ref[...] = jnp.where(iota((1, slots), 1) < count_ref[0], raw, 0.0)


def partners(turn, bits, tm_count, lat_count):
    pairs = []
    for tm in range(tm_count):
        for lat in range(lat_count):
            bit = bit_order(lat, bits)[turn]
            pairs.append((tm * lat_count + lat, (tm ^ (1 << bit)) * lat_count + lat))
    return pairs


def edge_pairs(step, far, bits, tm_count, lat_count):
    pairs = []
    for tm in range(tm_count):
        for lat in range(lat_count):
            target = lat + step
            if 0 <= target < lat_count:
                other = tm ^ (1 << bit_order(target, bits)[0]) if far else tm
                pairs.append((tm * lat_count + lat, other * lat_count + target))
    return pairs


def local(wind_east, wind_north, snap_counts, snap_ids):
    slots, rows, lon_count = wind_east.shape
    tm_count, lat_count = lax.axis_size("tm"), lax.axis_size("lat")
    bits = tm_count.bit_length() - 1
    wide = RANK * rows
    cell_total = rows * lat_count * lon_count
    width = padded_width(lon_count)
    east = wind_east.reshape(slots * rows, lon_count)
    north = wind_north.reshape(slots * rows, lon_count)
    both = ("tm", "lat")
    float_array = lambda *shape: jax.ShapeDtypeStruct(shape, jnp.float32)
    half_array = lambda *shape: jax.ShapeDtypeStruct(shape, jnp.bfloat16)

    outputs = pl.pallas_call(
        functools.partial(sketch_kernel, rows, lon_count),
        in_specs=[SCALARS, FAR, FAR, FAR],
        out_specs=[WHOLE] * 6,
        out_shape=[half_array(wide // 2, lon_count), float_array(wide // 2, lon_count)]
        + [half_array(RANK // 2, lon_count)] * 4,
        scratch_shapes=[
            pltpu.VMEM((wide, slots * rows), jnp.bfloat16),
            pltpu.VMEM((1, slots), jnp.int32),
            pltpu.VMEM((slots * rows, lon_count), jnp.bfloat16),
            pltpu.VMEM((slots * rows, lon_count), jnp.bfloat16),
            pltpu.VMEM((wide, width), jnp.float32),
            pltpu.VMEM((wide, width), jnp.float32),
            pltpu.SemaphoreType.DMA((5,)),
        ],
        compiler_params=params(),
        name="sketch_terms",
    )(snap_counts, in_hbm(snap_ids.reshape(1, slots)), in_hbm(east), in_hbm(north))
    send, keep, up_near, up_far, down_near, down_far = outputs

    got = lax.ppermute(send, both, partners(0, bits, tm_count, lat_count))
    edges = [
        lax.ppermute(up_near, both, edge_pairs(1, False, bits, tm_count, lat_count)),
        lax.ppermute(up_far, both, edge_pairs(1, True, bits, tm_count, lat_count)),
        lax.ppermute(down_near, both, edge_pairs(-1, False, bits, tm_count, lat_count)),
        lax.ppermute(down_far, both, edge_pairs(-1, True, bits, tm_count, lat_count)),
    ]
    send, keep = pl.pallas_call(
        functools.partial(halo_kernel, rows),
        in_specs=[WHOLE] * 6,
        out_specs=[WHOLE, WHOLE],
        out_shape=[half_array(wide // 4, lon_count), float_array(wide // 4, lon_count)],
        compiler_params=params(),
        name="halo_terms",
    )(keep, got, *edges)

    edge_source, send = lax.optimization_barrier((wind_east, send))
    wind_above = lax.ppermute(edge_source[:, rows - 1, :], both, edge_pairs(1, False, bits, tm_count, lat_count))
    wind_below = lax.ppermute(edge_source[:, 0, :], both, edge_pairs(-1, False, bits, tm_count, lat_count))

    for turn in range(1, bits):
        got = lax.ppermute(send, both, partners(turn, bits, tm_count, lat_count))
        if turn == bits - 1:
            got, wind_above, wind_below = lax.optimization_barrier((got, wind_above, wind_below))
        keep = keep + got.astype(jnp.float32)
        if turn < bits - 1:
            half = keep.shape[0] // 2
            send, keep = keep[half:].astype(jnp.bfloat16), keep[:half]
    held = keep.astype(jnp.bfloat16)
    piece_rows = held.shape[0]
    for turn in reversed(range(1, bits)):
        got = lax.ppermute(held, both, partners(turn, bits, tm_count, lat_count))
        held = jnp.concatenate([held, got], axis=0)
    got = lax.ppermute(held, both, partners(0, bits, tm_count, lat_count))

    terms_width = -(-slots // 128) * 128

    def project(piece):
        tall = piece.shape[0]
        return pl.pallas_call(
            functools.partial(project_kernel, rows, lon_count),
            in_specs=[WHOLE] * 5,
            out_specs=WHOLE,
            out_shape=float_array(tall // rows, terms_width),
            scratch_shapes=[
                pltpu.VMEM((tall, width), jnp.float32),
                pltpu.VMEM((tall, lon_count), jnp.bfloat16),
                pltpu.VMEM((tall, lon_count), jnp.bfloat16),
            ],
            cost_estimate=pl.CostEstimate(
                flops=4 * tall * slots * rows * lon_count,
                bytes_accessed=4 * slots * rows * lon_count,
                transcendentals=0,
            ),
            compiler_params=params(),
            name="projection_terms",
        )(piece, wind_above, wind_below, east, north)

    head, tail = project(held), project(got)
    sketch, sums = pl.pallas_call(
        functools.partial(gather_kernel, rows, piece_rows),
        in_specs=[WHOLE] * 4,
        out_specs=[WHOLE, WHOLE],
        out_shape=[half_array(wide, lon_count), float_array(RANK, terms_width + 128)],
        compiler_params=params(),
        name="gram_terms",
    )(held, got, head, tail)

    shift = 1
    while shift < lat_count:
        sums = sums + lax.ppermute(sums, "lat", [(i, i ^ shift) for i in range(lat_count)])
        shift *= 2

    basis, coeffs = pl.pallas_call(
        functools.partial(solve_kernel, rows, cell_total),
        in_specs=[SCALARS, WHOLE, WHOLE],
        out_specs=[WHOLE, WHOLE],
        out_shape=[half_array(wide, lon_count), float_array(RANK, slots)],
        scratch_shapes=[pltpu.VMEM((RANK, 128), jnp.float32)],
        compiler_params=params(),
        name="basis_and_coeffs",
    )(snap_counts, sums, sketch)
    return basis.reshape(RANK, rows, lon_count), coeffs


def solution(mesh):
    in_specs = (P("tm", "lat", None), P("tm", "lat", None), P("tm"), P("tm"))
    out_specs = (P(None, "lat", None), P(None, "tm"))
    return jax.shard_map(local, mesh=mesh, in_specs=in_specs, out_specs=out_specs, check_vma=False)
```

time: 73.7 us -> 72.1 us (0.978)
  waiting for transfers between devices: 34.1 us -> 31.1 us
  starting transfers between devices: 21.1 us -> 23.9 us
  Pallas kernels: 15.5 us -> 14.3 us
    ppermute x4 -> x8, starting transfers between devices: 10.5 us -> 19.5 us  [the longest x1 5.09 us: local(): lax.ppermute(up_far, both, edge_pairs(1, True, bits, tm_count, lat_count))]
    ppermute x4 -> x8, waiting for transfers between devices: 2.15 us -> 7.75 us  [the longest x1 3.65 us: local(): got = lax.ppermute(held, both, partners(0, bits, tm_count, lat_count))]
    ppermute x3 -> x2, waiting for transfers between devices: 18.7 us -> 13.3 us  [local(): got = lax.ppermute(held, both, partners(turn, bits, tm_count, lat_count))]
    ppermute x3 -> x2, waiting for transfers between devices: 10.2 us -> 5.74 us  [local(): got = lax.ppermute(send, both, partners(turn, bits, tm_count, lat_count))]
    ppermute x2, starting transfers between devices: 3.4 us -> 0.84 us  [local(): lax.ppermute(sums, 'lat', [(i, i ^ shift) for i in range(lat_count)])]
    ppermute x3 -> x2, starting transfers between devices: 2.39 us -> 0.36 us  [local(): got = lax.ppermute(held, both, partners(turn, bits, tm_count, lat_count))]
    ppermute x3 -> x2, starting transfers between devices: 4.73 us -> 3.17 us  [local(): got = lax.ppermute(send, both, partners(turn, bits, tm_count, lat_count))]
    ppermute x2, waiting for transfers between devices: 3.13 us -> 4.31 us  [local(): lax.ppermute(sums, 'lat', [(i, i ^ shift) for i in range(lat_count)])]
  transfers between devices with their start and end apart: 12 -> 14, of which waited for: 9 -> 8; matrix products, arithmetic and copies ran while one was open for 1% -> 1% of each run, Pallas kernels for 3% -> 4%
where the time goes in v3:
time: 72.1 us; the launch traced here: 71.8 us
  waiting for transfers between devices  31.1 us (43%)
  starting transfers between devices  23.9 us (33%)
  Pallas kernels  14.3 us (20%)
  between operations  1.44 us (2%)
  local copies, waits for them, and re-layouts  0.94 us (1%)
    ppermute x2, waiting for transfers between devices, local(): got = lax.ppermute(held, both, partners(turn, bits, tm_count, lat_count))  13.3 us
    ppermute x2, waiting for transfers between devices, local(): got = lax.ppermute(send, both, partners(turn, bits, tm_count, lat_count))  5.74 us
    pallas_call x2, Pallas kernels, project(): pl.pallas_call(functools.partial(project_kernel, rows, lon_count), in_spe...  5.59 us
    ppermute x1, starting transfers between devices, local(): lax.ppermute(up_far, both, edge_pairs(1, True, bits, tm_count, lat_count))  5.09 us
    pallas_call x1, Pallas kernels, local(): pl.pallas_call(functools.partial(sketch_kernel, rows, lon_count), in_spec...  4.93 us
    ppermute x1, starting transfers between devices, local(): lax.ppermute(edge_source[:, rows - 1, :], both, edge_pairs(1, False, bits...  4.38 us
    ppermute x2, waiting for transfers between devices, local(): lax.ppermute(sums, 'lat', [(i, i ^ shift) for i in range(lat_count)])  4.31 us
    ppermute x1, waiting for transfers between devices, local(): got = lax.ppermute(held, both, partners(0, bits, tm_count, lat_count))  3.65 us
  transfers between devices with their start and end apart: 14, of which 8 were waited for; matrix products, arithmetic and copies ran while one was open for 1% of the time, Pallas kernels for 4%

profile of v3, /device:TPU:0, one launch (start us, length us, event | category | flops | bytes accessed | tf_op | source)
XLA Modules:
  0.0 71.8 jit_solution(7535859231614821555)
XLA Ops:
  1.3 0.0 copy-start
  1.3 4.9 %sketch_terms.1 = (bf16[128,1440]{1,0:T(8,128)(2,1)S(1)}, f32[128,1440]{1,0:T(8,128)S(1)}, bf16[16,1440]{1,0:T(8,128)(2,1)S(1)}, bf16[16,1440]{1,0:T(8,128)(2,1)...) custom-call(s32[1]{0:T(128)S(6)} %copy.8.count_ref, s32[1,120]{1,0:T(1,128)} %bitcast.14, ...), custom_call_target="tpu_custom_call" | custom-call | tf_op jit(solution)/shard_map/sketch_terms/pallas_call | solution.py:344
  6.2 3.0 %collective-permute-start = (bf16[128,1440]{1,0:T(8,128)(2,1)S(1)}, bf16[128,1440]{1,0:T(8,128)(2,1)S(1)}, u32[]{:S(2)}, u32[]{:S(2)}) collective-permute-start(bf16[128,1440]{1,0:T(8,128)(2,1)S(1)} %get-tuple-element.20), channel_id=1, source_target_pairs={{0,4},{1,9},{2,6},{3,11},{4,0},{5,13},{6,2},{7,15},{8,12},{9,1},{1... | collective-permute-start | bytes 1105928 | tf_op jit(solution)/shard_map/ppermute | solution.py:364
  9.2 1.5 %collective-permute-start.1 = (bf16[16,1440]{1,0:T(8,128)(2,1)S(1)}, bf16[16,1440]{1,0:T(8,128)(2,1)S(1)}, u32[]{:S(2)}, u32[]{:S(2)}) collective-permute-start(bf16[16,1440]{1,0:T(8,128)(2,1)S(1)} %get-tuple-element.21), channel_id=1, source_target_pairs={{0,1},{1,2},{2,3},{4,5},{5,6},{6,7},{8,9},{9,10},{10,11},{12,13},{... | collective-permute-start | bytes 138248 | tf_op jit(solution)/shard_map/ppermute | solution.py:366
  10.8 5.1 %collective-permute-start.2 = (bf16[16,1440]{1,0:T(8,128)(2,1)S(1)}, bf16[16,1440]{1,0:T(8,128)(2,1)S(1)}, u32[]{:S(2)}, u32[]{:S(2)}) collective-permute-start(bf16[16,1440]{1,0:T(8,128)(2,1)S(1)} %get-tuple-element.22), channel_id=1, source_target_pairs={{0,9},{1,6},{2,11},{4,13},{5,2},{6,15},{8,1},{9,14},{10,3},{12,5},... | collective-permute-start | bytes 138248 | tf_op jit(solution)/shard_map/ppermute | solution.py:367
  15.9 1.3 %collective-permute-start.3 = (bf16[16,1440]{1,0:T(8,128)(2,1)S(1)}, bf16[16,1440]{1,0:T(8,128)(2,1)S(1)}, u32[]{:S(2)}, u32[]{:S(2)}) collective-permute-start(bf16[16,1440]{1,0:T(8,128)(2,1)S(1)} %get-tuple-element.23), channel_id=1, source_target_pairs={{1,0},{2,1},{3,2},{5,4},{6,5},{7,6},{9,8},{10,9},{11,10},{13,12},{... | collective-permute-start | bytes 138248 | tf_op jit(solution)/shard_map/ppermute | solution.py:368
  17.2 1.3 %collective-permute-start.4 = (bf16[16,1440]{1,0:T(8,128)(2,1)S(1)}, bf16[16,1440]{1,0:T(8,128)(2,1)S(1)}, u32[]{:S(2)}, u32[]{:S(2)}) collective-permute-start(bf16[16,1440]{1,0:T(8,128)(2,1)S(1)} %get-tuple-element.24), channel_id=1, source_target_pairs={{1,4},{2,9},{3,6},{5,0},{6,13},{7,2},{9,12},{10,1},{11,14},{13,8},... | collective-permute-start | bytes 138248 | tf_op jit(solution)/shard_map/ppermute | solution.py:369
  18.5 0.0 collective-permute-done.1.up_near
  18.5 0.0 collective-permute-done.2.up_far
  18.5 0.5 collective-permute-done.3.down_near
  19.0 3.6 %collective-permute-done.4.down_far = bf16[16,1440]{1,0:T(8,128)(2,1)S(1)} collective-permute-done((bf16[16,1440]{1,0:T(8,128)(2,1)S(1)}, bf16[16,1440]{1,0:T(8,128)(2,1)S(1)}, u32[]{:S(2)}, u32[]{:S(2)}) %collective-permute-start.4) | collective-permute-done | bytes 46112 | tf_op jit(solution)/shard_map/ppermute | solution.py:369
  22.6 0.0 collective-permute-done.got_ref
  22.6 0.3 halo_terms.1
  22.8 0.5 collective-permute-start.5
  23.4 0.0 copy-done
  23.4 0.9 %copy.6 = bf16[120,8,1440]{2,0,1:T(8,128)(2,1)S(1)} copy(bf16[120,8,1440]{2,1,0:T(8,128)(2,1)S(1)} %copy-done) | data formatting | bytes 5529600 | tf_op jit(solution)/shard_map/optimization_barrier | solution.py:380
  24.2 0.0 copy-start.1
  24.2 0.1 slice_bitcast_fusion
  24.3 1.6 %collective-permute-start.8 = (bf16[120,1440]{1,0:T(8,128)(2,1)S(1)}, bf16[120,1440]{1,0:T(8,128)(2,1)S(1)}, u32[]{:S(2)}, u32[]{:S(2)}) collective-permute-start(bf16[120,1440]{1,0:T(8,128)(2,1)S(1)} %get-tuple-element.36), channel_id=1, source_target_pairs={{1,0},{2,1},{3,2},{5,4},{6,5},{7,6},{9,8},{10,9},{11,10},{13,12},{... | collective-permute-start | bytes 1036808 | tf_op jit(solution)/shard_map/ppermute | solution.py:382
  25.9 4.4 %collective-permute-start.7 = (bf16[120,1440]{1,0:T(8,128)(2,1)S(1)}, bf16[120,1440]{1,0:T(8,128)(2,1)S(1)}, u32[]{:S(2)}, u32[]{:S(2)}) collective-permute-start(bf16[120,1440]{1,0:T(8,128)(2,1)S(1)} %get-tuple-element.37), channel_id=1, source_target_pairs={{0,1},{1,2},{2,3},{4,5},{5,6},{6,7},{8,9},{9,10},{10,11},{12,13},{... | collective-permute-start | bytes 1036808 | tf_op jit(solution)/shard_map/ppermute | solution.py:381
  30.3 0.0 collective-permute-done.5
  30.3 2.7 %collective-permute-start.6 = (bf16[32,1440]{1,0:T(8,128)(2,1)S(1)}, bf16[32,1440]{1,0:T(8,128)(2,1)S(1)}, u32[]{:S(2)}, u32[]{:S(2)}) collective-permute-start(bf16[32,1440]{1,0:T(8,128)(2,1)S(1)} %slice.27), channel_id=1, source_target_pairs={{0,16},{1,17},{2,18},{3,19},{4,20},{5,21},{6,22},{7,23},{8,24},{9,... | collective-permute-start | bytes 276488 | tf_op jit(solution)/shard_map/ppermute | solution.py:385
  33.0 5.7 %collective-permute-done.6 = bf16[32,1440]{1,0:T(8,128)(2,1)S(1)} collective-permute-done((bf16[32,1440]{1,0:T(8,128)(2,1)S(1)}, bf16[32,1440]{1,0:T(8,128)(2,1)S(1)}, u32[]{:S(2)}, u32[]{:S(2)}) %collective-permute-start.6) | collective-permute-done | bytes 92192 | tf_op jit(solution)/shard_map/ppermute | solution.py:385
  38.7 0.0 collective-permute-done.8.down_ref
  38.7 0.0 collective-permute-done.7.up_ref
  38.8 0.3 collective-permute-start.9
  39.0 7.6 %collective-permute-done.9 = bf16[32,1440]{1,0:T(8,128)(2,1)S(1)} collective-permute-done((bf16[32,1440]{1,0:T(8,128)(2,1)S(1)}, bf16[32,1440]{1,0:T(8,128)(2,1)S(1)}, u32[]{:S(2)}, u32[]{:S(2)}) %collective-permute-start.9) | collective-permute-done | bytes 92192 | tf_op jit(solution)/shard_map/ppermute | solution.py:395
  46.7 0.1 collective-permute-start.10
  46.8 5.7 %collective-permute-done.10 = bf16[64,1440]{1,0:T(8,128)(2,1)S(1)} collective-permute-done((bf16[64,1440]{1,0:T(8,128)(2,1)S(1)}, bf16[64,1440]{1,0:T(8,128)(2,1)S(1)}, u32[]{:S(2)}, u32[]{:S(2)}) %collective-permute-start.10) | collective-permute-done | bytes 184352 | tf_op jit(solution)/shard_map/ppermute | solution.py:395
  52.5 1.4 %collective-permute-start.11 = (bf16[128,1440]{1,0:T(8,128)(2,1)S(1)}, bf16[128,1440]{1,0:T(8,128)(2,1)S(1)}, u32[]{:S(2)}, u32[]{:S(2)}) collective-permute-start(bf16[128,1440]{1,0:T(8,128)(2,1)S(1)} %pad_maximum_fusion.piece_ref.first_ref), channel_id=1, source_target_pairs={{0,4},{1,9},{2,6},{3,11},{4,0},{5,13},{6,2},{7,15},{8,12},{9,1},{1... | collective-permute-start | bytes 1105928 | tf_op jit(solution)/shard_map/ppermute | solution.py:397
  53.9 0.0 copy-done.1
  53.9 2.8 %projection_terms.2.head_ref = f32[16,128]{1,0:T(8,128)S(1)} custom-call(bf16[128,1440]{1,0:T(8,128)(2,1)S(1)} %pad_maximum_fusion.piece_ref.first_ref, bf16[120,1440]{1,0:T(8,128)(2,1)S(1)} %collective-permute-done.7.up_ref, bf16[120,1440]{1,0:T(8,128)(2,1)S(1)} %collective-permute-done.8.down_ref, bf16[960,1440]{1,0:T(8,128)(2,1)S(1)} %bitcast.9, ...), custom_call_target="tpu_custom_call" | custom-call | flops 707788800 | bytes 5529600 | tf_op jit(solution)/shard_map/projection_terms/pallas_call | solution.py:403
  56.7 3.7 %collective-permute-done.11.piece_ref.second_ref = bf16[128,1440]{1,0:T(8,128)(2,1)S(1)} collective-permute-done((bf16[128,1440]{1,0:T(8,128)(2,1)S(1)}, bf16[128,1440]{1,0:T(8,128)(2,1)S(1)}, u32[]{:S(2)}, u32[]{:S(2)}) %collective-permute-start.11) | collective-permute-done | bytes 368672 | tf_op jit(solution)/shard_map/ppermute | solution.py:397
  60.3 2.8 %projection_terms.3.tail_ref = f32[16,128]{1,0:T(8,128)S(1)} custom-call(bf16[128,1440]{1,0:T(8,128)(2,1)S(1)} %collective-permute-done.11.piece_ref.second_ref, bf16[120,1440]{1,0:T(8,128)(2,1)S(1)} %collective-permute-done.7.up_ref, bf16[120,1440]{1,0:T(8,128)(2,1)S(1)} %collective-permute-done.8.down_ref, bf16[960,1440]{1,0:T(8,128)(2,1)S(1)} %bitcast.10, ...), custom_call_target="tpu_custom_call" | custom-call | flops 707788800 | bytes 5529600 | tf_op jit(solution)/shard_map/projection_terms/pallas_call | solution.py:403
  63.1 0.8 %gram_terms.1 = (bf16[256,1440]{1,0:T(8,128)(2,1)S(1)}, f32[32,256]{1,0:T(8,128)S(1)}) custom-call(bf16[128,1440]{1,0:T(8,128)(2,1)S(1)} %pad_maximum_fusion.piece_ref.first_ref, bf16[128,1440]{1,0:T(8,128)(2,1)S(1)} %collective-permute-done.11.piece_ref.second_ref, f32[16,128]{1,0:T(8,128)S(1)} %projection_terms.2.head_ref, ...), custom_call_target="tpu_custom_call" | custom-call | tf_op jit(solution)/shard_map/gram_terms/pallas_call | solution.py:423
  63.9 0.0 collective-permute-start.12
  63.9 1.2 %collective-permute-done.12 = f32[32,256]{1,0:T(8,128)S(1)} collective-permute-done((f32[32,256]{1,0:T(8,128)S(1)}, f32[32,256]{1,0:T(8,128)S(1)}, u32[]{:S(2)}, u32[]{:S(2)}) %collective-permute-start.12) | collective-permute-done | bytes 32800 | tf_op jit(solution)/shard_map/ppermute | solution.py:434
  65.1 0.8 %collective-permute-start.13 = (f32[32,256]{1,0:T(8,128)S(1)}, f32[32,256]{1,0:T(8,128)S(1)}, u32[]{:S(2)}, u32[]{:S(2)}) collective-permute-start(f32[32,256]{1,0:T(8,128)S(1)} %add.14), channel_id=1, source_target_pairs={{0,2},{1,3},{2,0},{3,1},{4,6},{5,7},{6,4},{7,5},{8,10},{9,11},{10,... | collective-permute-start | bytes 98312 | tf_op jit(solution)/shard_map/ppermute | solution.py:434
  66.0 3.1 %collective-permute-done.13 = f32[32,256]{1,0:T(8,128)S(1)} collective-permute-done((f32[32,256]{1,0:T(8,128)S(1)}, f32[32,256]{1,0:T(8,128)S(1)}, u32[]{:S(2)}, u32[]{:S(2)}) %collective-permute-start.13) | collective-permute-done | bytes 32800 | tf_op jit(solution)/shard_map/ppermute | solution.py:434
  69.0 2.8 %basis_and_coeffs.1 = (bf16[256,1440]{1,0:T(8,128)(2,1)}, f32[32,120]{1,0:T(8,128)}) custom-call(s32[1]{0:T(128)S(6)} %copy.8.count_ref, f32[32,256]{1,0:T(8,128)S(1)} %add.15.sums_ref, bf16[256,1440]{1,0:T(8,128)(2,1)S(1)} %get-tuple-element.33.sketch_ref), custom_call_target="tpu_custom_call" | custom-call | tf_op jit(solution)/shard_map/basis_and_coeffs/pallas_call | solution.py:437
  (7 shorter events, 0.1 us)
Async XLA Ops:
  1.3 22.1 %copy-start = (bf16[120,8,1440]{2,1,0:T(8,128)(2,1)S(1)}, bf16[120,8,1440]{2,1,0:T(8,128)(2,1)}, u32[]{:S(2)}) copy-start(bf16[120,8,1440]{2,1,0:T(8,128)(2,1)} %param.4) | copy-start | bytes 8294404
  6.2 16.4 %collective-permute-start = (bf16[128,1440]{1,0:T(8,128)(2,1)S(1)}, bf16[128,1440]{1,0:T(8,128)(2,1)S(1)}, u32[]{:S(2)}, u32[]{:S(2)}) collective-permute-start(bf16[128,1440]{1,0:T(8,128)(2,1)S(1)} %get-tuple-element.20), channel_id=1, source_target_pairs={{0,4},{1,9},{2,6},{3,11},{4,0},{5,13},{6,2},{7,15},{8,12},{9,1},{1... | collective-permute-start | bytes 1105928 | tf_op jit(solution)/shard_map/ppermute | solution.py:364
  9.2 9.2 %collective-permute-start.1 = (bf16[16,1440]{1,0:T(8,128)(2,1)S(1)}, bf16[16,1440]{1,0:T(8,128)(2,1)S(1)}, u32[]{:S(2)}, u32[]{:S(2)}) collective-permute-start(bf16[16,1440]{1,0:T(8,128)(2,1)S(1)} %get-tuple-element.21), channel_id=1, source_target_pairs={{0,1},{1,2},{2,3},{4,5},{5,6},{6,7},{8,9},{9,10},{10,11},{12,13},{... | collective-permute-start | bytes 138248 | tf_op jit(solution)/shard_map/ppermute | solution.py:366
  10.8 7.7 %collective-permute-start.2 = (bf16[16,1440]{1,0:T(8,128)(2,1)S(1)}, bf16[16,1440]{1,0:T(8,128)(2,1)S(1)}, u32[]{:S(2)}, u32[]{:S(2)}) collective-permute-start(bf16[16,1440]{1,0:T(8,128)(2,1)S(1)} %get-tuple-element.22), channel_id=1, source_target_pairs={{0,9},{1,6},{2,11},{4,13},{5,2},{6,15},{8,1},{9,14},{10,3},{12,5},... | collective-permute-start | bytes 138248 | tf_op jit(solution)/shard_map/ppermute | solution.py:367
  15.9 3.1 %collective-permute-start.3 = (bf16[16,1440]{1,0:T(8,128)(2,1)S(1)}, bf16[16,1440]{1,0:T(8,128)(2,1)S(1)}, u32[]{:S(2)}, u32[]{:S(2)}) collective-permute-start(bf16[16,1440]{1,0:T(8,128)(2,1)S(1)} %get-tuple-element.23), channel_id=1, source_target_pairs={{1,0},{2,1},{3,2},{5,4},{6,5},{7,6},{9,8},{10,9},{11,10},{13,12},{... | collective-permute-start | bytes 138248 | tf_op jit(solution)/shard_map/ppermute | solution.py:368
  17.2 5.4 %collective-permute-start.4 = (bf16[16,1440]{1,0:T(8,128)(2,1)S(1)}, bf16[16,1440]{1,0:T(8,128)(2,1)S(1)}, u32[]{:S(2)}, u32[]{:S(2)}) collective-permute-start(bf16[16,1440]{1,0:T(8,128)(2,1)S(1)} %get-tuple-element.24), channel_id=1, source_target_pairs={{1,4},{2,9},{3,6},{5,0},{6,13},{7,2},{9,12},{10,1},{11,14},{13,8},... | collective-permute-start | bytes 138248 | tf_op jit(solution)/shard_map/ppermute | solution.py:369
  22.8 7.4 %collective-permute-start.5 = (bf16[64,1440]{1,0:T(8,128)(2,1)S(1)}, bf16[64,1440]{1,0:T(8,128)(2,1)S(1)}, u32[]{:S(2)}, u32[]{:S(2)}) collective-permute-start(bf16[64,1440]{1,0:T(8,128)(2,1)S(1)} %get-tuple-element.27), channel_id=1, source_target_pairs={{0,8},{1,5},{2,10},{3,7},{4,12},{5,1},{6,14},{7,3},{8,0},{9,13},{1... | collective-permute-start | bytes 552968 | tf_op jit(solution)/shard_map/ppermute | solution.py:385
  24.2 29.7 %copy-start.1 = (bf16[120,8,1440]{2,1,0:T(8,128)(2,1)S(1)}, bf16[120,8,1440]{2,1,0:T(8,128)(2,1)}, u32[]{:S(2)}) copy-start(bf16[120,8,1440]{2,1,0:T(8,128)(2,1)} %param.5) | copy-start | bytes 8294404
  24.3 14.4 %collective-permute-start.8 = (bf16[120,1440]{1,0:T(8,128)(2,1)S(1)}, bf16[120,1440]{1,0:T(8,128)(2,1)S(1)}, u32[]{:S(2)}, u32[]{:S(2)}) collective-permute-start(bf16[120,1440]{1,0:T(8,128)(2,1)S(1)} %get-tuple-element.36), channel_id=1, source_target_pairs={{1,0},{2,1},{3,2},{5,4},{6,5},{7,6},{9,8},{10,9},{11,10},{13,12},{... | collective-permute-start | bytes 1036808 | tf_op jit(solution)/shard_map/ppermute | solution.py:382
  25.9 12.9 %collective-permute-start.7 = (bf16[120,1440]{1,0:T(8,128)(2,1)S(1)}, bf16[120,1440]{1,0:T(8,128)(2,1)S(1)}, u32[]{:S(2)}, u32[]{:S(2)}) collective-permute-start(bf16[120,1440]{1,0:T(8,128)(2,1)S(1)} %get-tuple-element.37), channel_id=1, source_target_pairs={{0,1},{1,2},{2,3},{4,5},{5,6},{6,7},{8,9},{9,10},{10,11},{12,13},{... | collective-permute-start | bytes 1036808 | tf_op jit(solution)/shard_map/ppermute | solution.py:381
  30.3 8.4 %collective-permute-start.6 = (bf16[32,1440]{1,0:T(8,128)(2,1)S(1)}, bf16[32,1440]{1,0:T(8,128)(2,1)S(1)}, u32[]{:S(2)}, u32[]{:S(2)}) collective-permute-start(bf16[32,1440]{1,0:T(8,128)(2,1)S(1)} %slice.27), channel_id=1, source_target_pairs={{0,16},{1,17},{2,18},{3,19},{4,20},{5,21},{6,22},{7,23},{8,24},{9,... | collective-permute-start | bytes 276488 | tf_op jit(solution)/shard_map/ppermute | solution.py:385
  38.8 7.9 %collective-permute-start.9 = (bf16[32,1440]{1,0:T(8,128)(2,1)S(1)}, bf16[32,1440]{1,0:T(8,128)(2,1)S(1)}, u32[]{:S(2)}, u32[]{:S(2)}) collective-permute-start(bf16[32,1440]{1,0:T(8,128)(2,1)S(1)} %fusion), channel_id=1, source_target_pairs={{0,16},{1,17},{2,18},{3,19},{4,20},{5,21},{6,22},{7,23},{8,24},{9,... | collective-permute-start | bytes 276488 | tf_op jit(solution)/shard_map/ppermute | solution.py:395
  46.7 5.7 %collective-permute-start.10 = (bf16[64,1440]{1,0:T(8,128)(2,1)S(1)}, bf16[64,1440]{1,0:T(8,128)(2,1)S(1)}, u32[]{:S(2)}, u32[]{:S(2)}) collective-permute-start(bf16[64,1440]{1,0:T(8,128)(2,1)S(1)} %pad_maximum_fusion.1), channel_id=1, source_target_pairs={{0,8},{1,5},{2,10},{3,7},{4,12},{5,1},{6,14},{7,3},{8,0},{9,13},{1... | collective-permute-start | bytes 552968 | tf_op jit(solution)/shard_map/ppermute | solution.py:395
  52.5 7.8 %collective-permute-start.11 = (bf16[128,1440]{1,0:T(8,128)(2,1)S(1)}, bf16[128,1440]{1,0:T(8,128)(2,1)S(1)}, u32[]{:S(2)}, u32[]{:S(2)}) collective-permute-start(bf16[128,1440]{1,0:T(8,128)(2,1)S(1)} %pad_maximum_fusion.piece_ref.first_ref), channel_id=1, source_target_pairs={{0,4},{1,9},{2,6},{3,11},{4,0},{5,13},{6,2},{7,15},{8,12},{9,1},{1... | collective-permute-start | bytes 1105928 | tf_op jit(solution)/shard_map/ppermute | solution.py:397
  63.9 1.2 %collective-permute-start.12 = (f32[32,256]{1,0:T(8,128)S(1)}, f32[32,256]{1,0:T(8,128)S(1)}, u32[]{:S(2)}, u32[]{:S(2)}) collective-permute-start(f32[32,256]{1,0:T(8,128)S(1)} %get-tuple-element.32), channel_id=1, source_target_pairs={{0,1},{1,0},{2,3},{3,2},{4,5},{5,4},{6,7},{7,6},{8,9},{9,8},{10,11... | collective-permute-start | bytes 98312 | tf_op jit(solution)/shard_map/ppermute | solution.py:434
  65.1 3.9 %collective-permute-start.13 = (f32[32,256]{1,0:T(8,128)S(1)}, f32[32,256]{1,0:T(8,128)S(1)}, u32[]{:S(2)}, u32[]{:S(2)}) collective-permute-start(f32[32,256]{1,0:T(8,128)S(1)} %add.14), channel_id=1, source_target_pairs={{0,2},{1,3},{2,0},{3,1},{4,6},{5,7},{6,4},{7,5},{8,10},{9,11},{10,... | collective-permute-start | bytes 98312 | tf_op jit(solution)/shard_map/ppermute | solution.py:434
